TPU v7x, 128 devices: a whole 4x4x4 slice. The times are simulated.
128 devices in a mesh: section: 2 (over x_lo), dp: 4 (over x_hi, core), mp: 16 (over y, z).
Axes of the slice: x: 4 (x_hi: 2, x_lo: 2; x = x_hi * 2 + x_lo), y: 4, z: 4, core: 2. Of those that a mesh axis runs over, the one named last changes fastest.
Arguments:
- late_inputs: bfloat16 [1024, 8192], P('dp'), may hold values from -6 to 6
- cotangent: bfloat16 [1024, 8192], P('dp'), may hold values from -6 to 6
- early_inputs: bfloat16 [1024, 8192], P('dp'), may hold values from -6 to 6
- doc_lengths: int32 [4, 4], P('dp'), may hold values from 1 to 128, 256 in all within a row
- norm_gain: bfloat16 [2, 8192], P('section'), may hold values from 0.5 to 1.5
- w_query: bfloat16 [2, 8192, 4096], P('section', None, 'mp'), may hold values from -0.0625 to 0.0625
- w_key: bfloat16 [2, 8192, 512], P('section', None, 'mp'), may hold values from -0.0625 to 0.0625
- w_value: bfloat16 [2, 8192, 512], P('section', None, 'mp'), may hold values from -0.0625 to 0.0625
- w_output: bfloat16 [2, 8192, 4096], P('section', None, 'mp'), may hold values from -0.09375 to 0.09375
Outputs:
- input_grads: bfloat16 [2, 1024, 8192], P('section', 'dp', 'mp')
- grad_query: bfloat16 [2, 8192, 4096], P('section', 'dp', 'mp')
- grad_key: bfloat16 [2, 8192, 512], P('section', 'dp', 'mp')
- grad_value: bfloat16 [2, 8192, 512], P('section', 'dp', 'mp')
- grad_output: bfloat16 [2, 8192, 4096], P('section', 'dp', 'mp')
Inputs may be any that keep to these rules, and one draw needn't show every extreme that they name: `doc_lengths`: each row lists the lengths of 4 documents that fill one sequence of 256 tokens.
All inputs are finite; a program needn't handle non-finite values.
Results may differ from a plain program's by a relative error of at most 0.028.
Values may be sent and summed in bfloat16 or wider, within the bound.
A program may use at most 192 MiB of HBM per device.

v0:
```python
import math

import jax
import jax.numpy as jnp
from jax import lax
from jax.sharding import PartitionSpec as P

HD = 128
HEADS = 32
KVH = 4


def passed_along(shard, axis, by):
    size = lax.axis_size(axis)
    pairs = [(i, i + by) for i in range(size) if 0 <= i + by < size]
    return lax.ppermute(shard, axis, pairs)


def swapped(shard, axis, stride):
    return lax.ppermute(shard, axis, [(i, i ^ 1 << stride) for i in range(lax.axis_size(axis))])


def doc_tables(lengths, seq_len, head_size):
    starts = jnp.cumsum(lengths) - lengths
    places = jnp.arange(seq_len, dtype=jnp.int32)
    begins = jnp.max(
        jnp.where(
            starts[None, :] <= places[:, None], starts[None, :], jnp.zeros_like(starts)[None, :]
        ),
        axis=1,
    )
    offsets = (places - begins).astype(jnp.float32)
    frequencies = 10000.0 ** (-jnp.arange(0, head_size, 2).astype(jnp.float32) / head_size)
    angles = offsets[:, None] * frequencies[None, :]
    cosine = jnp.concatenate([jnp.cos(angles), jnp.cos(angles)], axis=1)
    sine_table = jnp.concatenate([jnp.sin(angles), jnp.sin(angles)], axis=1)
    allowed = (begins[:, None] == begins[None, :]) & (places[None, :] <= places[:, None])
    return (cosine, sine_table, allowed)


def rotate(values):
    half_size = values.shape[-1] // 2
    return jnp.concatenate([-values[..., half_size:], values[..., :half_size]], axis=-1)


def apply_rope(values, cosine, sine_table):
    return values * cosine + rotate(values) * sine_table


def undo_rope(values, cosine, sine_table):
    return values * cosine - rotate(values * sine_table)


def batch_mix(pattern, first_op, second_op):
    return jnp.einsum(pattern, first_op, second_op, preferred_element_type=jnp.float32)


def matmul_nt(first_op, second_op):
    return lax.dot_general(
        first_op, second_op, (((1,), (1,)), ((), ())), preferred_element_type=jnp.float32
    )


def matmul_tn(first_op, second_op):
    return lax.dot_general(
        first_op, second_op, (((0,), (0,)), ((), ())), preferred_element_type=jnp.float32
    )


def head_block(
    tokens, upstream, norm_weight, w_query, w_key, w_value, w_output, cosine, sine_table, allowed
):
    seq_len = tokens.shape[0]
    head_size = cosine.shape[1]
    query_heads = w_query.shape[1] // head_size
    key_heads = w_key.shape[1] // head_size
    repeats = query_heads // key_heads
    score_scale = 1.0 / math.sqrt(head_size)
    cos_rows = cosine[:, None, :]
    sin_rows = sine_table[:, None, :]
    token_f32 = tokens.astype(jnp.float32)
    gain_f32 = norm_weight.astype(jnp.float32)
    inv_rms = lax.rsqrt(jnp.mean(token_f32 * token_f32, axis=1) + 1e-05)
    normed = (token_f32 * inv_rms[:, None] * gain_f32).astype(jnp.bfloat16)
    queries = apply_rope(
        jnp.dot(normed, w_query, preferred_element_type=jnp.float32).reshape(
            seq_len, query_heads, head_size
        ),
        cos_rows,
        sin_rows,
    ).astype(jnp.bfloat16)
    key_rows = apply_rope(
        jnp.dot(normed, w_key, preferred_element_type=jnp.float32).reshape(
            seq_len, key_heads, head_size
        ),
        cos_rows,
        sin_rows,
    ).astype(jnp.bfloat16)
    value_rows = (
        jnp.dot(normed, w_value, preferred_element_type=jnp.float32)
        .astype(jnp.bfloat16)
        .reshape(seq_len, key_heads, head_size)
    )
    key_wide = jnp.repeat(key_rows, repeats, axis=1)
    value_wide = jnp.repeat(value_rows, repeats, axis=1)
    scores = batch_mix("thd,shd->hts", queries, key_wide) * score_scale
    scores = jnp.where(allowed[None, :, :], scores, -1e30)
    row_peak = jnp.max(scores, axis=2, keepdims=True)
    exp_scores = jnp.exp(scores - row_peak)
    probs = exp_scores / jnp.sum(exp_scores, axis=2, keepdims=True)
    probs_low = probs.astype(jnp.bfloat16)
    context = batch_mix("hts,shd->thd", probs_low, value_wide).astype(jnp.bfloat16)
    grad_context = (
        jnp.dot(upstream, w_output, preferred_element_type=jnp.float32)
        .astype(jnp.bfloat16)
        .reshape(seq_len, query_heads, head_size)
    )
    grad_probs = batch_mix("thd,shd->hts", grad_context, value_wide)
    grad_scores = (
        probs * (grad_probs - jnp.sum(grad_probs * probs, axis=2, keepdims=True)) * score_scale
    ).astype(jnp.bfloat16)
    grad_queries = undo_rope(
        batch_mix("hts,shd->thd", grad_scores, key_wide), cos_rows, sin_rows
    ).astype(jnp.bfloat16)
    key_sum = (
        batch_mix("hts,thd->shd", grad_scores, queries)
        .reshape(seq_len, key_heads, repeats, head_size)
        .sum(axis=2)
    )
    key_part = undo_rope(key_sum, cos_rows, sin_rows).astype(jnp.bfloat16)
    value_part = (
        batch_mix("hts,thd->shd", probs_low, grad_context)
        .reshape(seq_len, key_heads, repeats, head_size)
        .sum(axis=2)
        .astype(jnp.bfloat16)
    )
    flat_query = grad_queries.reshape(seq_len, query_heads * head_size)
    flat_key = key_part.reshape(seq_len, key_heads * head_size)
    flat_value = value_part.reshape(seq_len, key_heads * head_size)
    grad_normed = (
        matmul_nt(flat_query, w_query) + matmul_nt(flat_key, w_key) + matmul_nt(flat_value, w_value)
    )
    stat_part = jnp.sum(token_f32 * gain_f32 * grad_normed, axis=1)
    return (
        grad_normed,
        stat_part,
        flat_key,
        flat_value,
        flat_query,
        context.reshape(seq_len, query_heads * head_size),
        normed,
        inv_rms,
    )


def reduce_heads(grad_normed, stat_cols, key_value):
    return (
        lax.psum_scatter(
            grad_normed.astype(jnp.bfloat16), "mp", scatter_dimension=1, tiled=True
        ).astype(jnp.float32),
        lax.psum_scatter(
            stat_cols.astype(jnp.bfloat16), "mp", scatter_dimension=1, tiled=True
        ).astype(jnp.float32),
        lax.psum_scatter(
            key_value.astype(jnp.bfloat16), "mp", scatter_dimension=1, tiled=True
        ).astype(jnp.float32),
    )


def send_back(values):
    return passed_along(values, "section", -1)


def collect(values):
    return lax.all_gather(values, "mp", axis=1, tiled=True)


def on_device(
    late_inputs, cotangent, early_inputs, doc_lengths, norm_gain, w_query, w_key, w_value, w_output
):
    section_index = lax.axis_index("section")
    column_index = lax.axis_index("mp")
    column_count = lax.axis_size("mp")
    seq_len, width = late_inputs.shape
    query_cols = w_query.shape[2]
    key_cols = w_key.shape[2]
    heads_here = query_cols // HD
    group_size = HEADS // KVH
    joined = jnp.stack([w_key[0], w_value[0]])
    halving = HD // key_cols
    for bit_number in range(halving.bit_length() - 1):
        partner = swapped(joined, "mp", bit_number)
        low_side = jnp.right_shift(column_index, bit_number) % 2 == 0
        joined = jnp.where(
            low_side,
            jnp.concatenate([joined, partner], axis=2),
            jnp.concatenate([partner, joined], axis=2),
        )
    cosine, sine_table, allowed = doc_tables(doc_lengths[0], seq_len, HD)
    key_start = column_index * heads_here // group_size * HD
    zero_index = jnp.zeros((), jnp.int32)
    norm_weight = norm_gain[0]
    tile_width = width // column_count
    tile_start = column_index * tile_width
    gain_tile = lax.dynamic_slice_in_dim(norm_weight, tile_start, tile_width, 0).astype(jnp.float32)

    def section_pass(tokens, upstream, active):

        def active_pass(unused):
            pieces = head_block(
                tokens,
                upstream,
                norm_weight,
                w_query[0],
                joined[0],
                joined[1],
                w_output[0],
                cosine,
                sine_table,
                allowed,
            )
            grad_normed, stat_part, key_grad, value_grad, query_grad, context, normed, inv_rms = (
                pieces
            )
            empty = jnp.zeros((seq_len, KVH * HD), jnp.float32)
            placed_key = lax.dynamic_update_slice(
                empty, key_grad.astype(jnp.float32), (zero_index, key_start)
            )
            placed_value = lax.dynamic_update_slice(
                empty, value_grad.astype(jnp.float32), (zero_index, key_start)
            )
            key_value = jnp.stack(
                [
                    placed_key.reshape(seq_len, column_count, key_cols),
                    placed_value.reshape(seq_len, column_count, key_cols),
                ],
                axis=2,
            ).reshape(seq_len, column_count * 2 * key_cols)
            stat_cols = jnp.broadcast_to(stat_part[:, None], (seq_len, column_count))
            return (grad_normed, stat_cols, key_value, normed, inv_rms, query_grad, context)

        def spare_pass(unused):
            return jax.tree.map(jnp.zeros_like, active_pass(unused))

        grad_normed, stat_cols, key_value, normed, inv_rms, query_grad, context = lax.cond(
            active, active_pass, spare_pass, 0
        )
        grad_tile, stat_tile, key_value_tile = reduce_heads(grad_normed, stat_cols, key_value)
        key_tile = key_value_tile[:, :key_cols].astype(jnp.bfloat16)
        value_tile = key_value_tile[:, key_cols:].astype(jnp.bfloat16)
        token_tile = lax.dynamic_slice_in_dim(tokens, tile_start, tile_width, 1).astype(jnp.float32)
        upstream_tile = lax.dynamic_slice_in_dim(upstream, tile_start, tile_width, 1).astype(
            jnp.float32
        )
        grad_in = (
            upstream_tile
            + inv_rms[:, None] * gain_tile * grad_tile
            - token_tile * (inv_rms**3 * stat_tile[:, 0] / width)[:, None]
        ).astype(jnp.bfloat16)
        return (grad_in, (normed, upstream, query_grad, context, key_tile, value_tile))

    is_later = section_index == 1
    late_grad, late_operands = section_pass(late_inputs, cotangent, is_later)
    arriving = send_back(collect(late_grad))
    early_grad, early_operands = section_pass(early_inputs, arriving, section_index == 0)
    grad_in = jnp.where(is_later, late_grad, early_grad)
    chosen = [
        jnp.where(is_later, late_part, early_part)
        for late_part, early_part in zip(late_operands, early_operands)
    ]
    normed, upstream, query_grad, context, key_tile, value_tile = chosen
    part_q = matmul_tn(normed, query_grad)
    part_k = matmul_tn(normed, key_tile)
    part_v = matmul_tn(normed, value_tile)
    part_o = matmul_tn(upstream, context)
    summed_q, summed_k, summed_v, summed_o = (
        lax.psum_scatter(part_q.astype(jnp.bfloat16), "dp", scatter_dimension=0, tiled=True).astype(
            jnp.float32
        ),
        lax.psum_scatter(part_k.astype(jnp.bfloat16), "dp", scatter_dimension=0, tiled=True).astype(
            jnp.float32
        ),
        lax.psum_scatter(part_v.astype(jnp.bfloat16), "dp", scatter_dimension=0, tiled=True).astype(
            jnp.float32
        ),
        lax.psum_scatter(part_o.astype(jnp.bfloat16), "dp", scatter_dimension=0, tiled=True).astype(
            jnp.float32
        ),
    )
    return (
        grad_in[None],
        summed_q.astype(jnp.bfloat16)[None],
        summed_k.astype(jnp.bfloat16)[None],
        summed_v.astype(jnp.bfloat16)[None],
        summed_o.astype(jnp.bfloat16)[None],
    )


def solution(mesh):
    in_specs = (
        P("dp", None),
        P("dp", None),
        P("dp", None),
        P("dp", None),
        P("section", None),
        P("section", None, "mp"),
        P("section", None, "mp"),
        P("section", None, "mp"),
        P("section", None, "mp"),
    )
    out_specs = (
        P("section", "dp", "mp"),
        P("section", "dp", "mp"),
        P("section", "dp", "mp"),
        P("section", "dp", "mp"),
        P("section", "dp", "mp"),
    )
    return jax.shard_map(
        on_device, mesh=mesh, in_specs=in_specs, out_specs=out_specs, check_vma=False
    )
```

profile of v0, /device:TPU:0, one launch (start us, length us, event | category | flops | bytes accessed | tf_op | source)
XLA Modules:
  0.0 756.0 jit_solution(11885057117760954008)
XLA Ops:
  11.5 23.3 %collective-permute-done = bf16[2,8192,32]{1,2,0:T(8,128)(2,1)} collective-permute-done((bf16[2,8192,32]{1,2,0:T(8,128)(2,1)S(1)}, bf16[2,8192,32]{1,2,0:T(8,128)(2,1)}, u32[]{:S(2)}, u32[]{:S(2)}) %collective-permute-start) | collective-permute-done | bytes 1048608 | tf_op jit(solution)/shard_map/ppermute | solution.py:20
  41.4 44.0 %collective-permute-done.1 = bf16[2,8192,64]{1,2,0:T(8,128)(2,1)} collective-permute-done((bf16[2,8192,64]{1,2,0:T(8,128)(2,1)S(1)}, bf16[2,8192,64]{1,2,0:T(8,128)(2,1)}, u32[]{:S(2)}, u32[]{:S(2)}) %collective-permute-start.1) | collective-permute-done | bytes 2097184 | tf_op jit(solution)/shard_map/ppermute | solution.py:20
  85.4 4.6 maximum_select_fusion
  90.0 9.6 %conditional.2 = (bf16[256,8192]{1,0:T(8,128)(2,1)}, bf16[256,16]{1,0:T(8,128)(2,1)S(1)}, bf16[256,1024]{0,1:T(8,128)(2,1)S(1)}, bf16[256,8192]{1,0:T(8,128)(2,1...) conditional(s32[]{:T(128)} %convert_element_type.203, () %tuple.28, ...), branch_computations={%region_2.3_spmd, %region_3.9_spmd} | conditional | flops 5671727104 | bytes 193544544 | solution.py:245
  100.9 75.5 %all-reduce = bf16[256,16]{1,0:T(8,128)(2,1)S(1)} all-reduce(bf16[256,16]{1,0:T(8,128)(2,1)S(1)} %get-tuple-element.86), channel_id=3, replica_groups=mesh['section'=2,'dp'=4,'mp'=16] {'mp'}, use_global_device_ids=true, to_apply=%region_10.11.clone | all-reduce | flops 4096 | bytes 16384
  177.2 45.1 %reduce-scatter.11.cloned.1.call-done = bf16[256,512]{1,0:T(8,128)(2,1)} async-done(((bf16[256,8192]{1,0:T(8,128)(2,1)}), bf16[256,512]{1,0:T(8,128)(2,1)}) %reduce-scatter.11.cloned.1.call-update) | async-done | bytes 262160 | tf_op jit(solution)/shard_map/reduce_scatter | solution.py:158
  224.4 57.7 %all-gather.2.cloned.1.call-done = bf16[256,8192]{1,0:T(8,128)(2,1)} async-done(((bf16[256,512]{1,0:T(8,128)(2,1)}), bf16[256,8192]{1,0:T(8,128)(2,1)}) %all-gather.2.cloned.1.call-update) | async-done | bytes 4194320 | tf_op jit(solution)/shard_map/all_gather | solution.py:175
  283.5 92.3 %collective-permute-done.2 = bf16[256,8192]{1,0:T(8,128)(2,1)} collective-permute-done((bf16[256,8192]{1,0:T(8,128)(2,1)}, bf16[256,8192]{1,0:T(8,128)(2,1)}, u32[]{:S(2)}, u32[]{:S(2)}) %collective-permute-start.2) | collective-permute-done | bytes 4194336 | tf_op jit(solution)/shard_map/ppermute | solution.py:16
  375.8 49.6 %conditional.3 = (bf16[256,8192]{1,0:T(8,128)(2,1)}, bf16[256,16]{1,0:T(8,128)(2,1)S(1)}, bf16[256,1024]{0,1:T(8,128)(2,1)S(1)}, bf16[256,8192]{1,0:T(8,128)(2,1...) conditional(s32[]{:T(128)} %convert_element_type.212, () %tuple.30, ...), branch_computations={%region_11.12_spmd, %region_12.18_spmd} | conditional | flops 5671727104 | bytes 174670144 | solution.py:245
  375.8 5.3 fusion.89
  385.2 6.5 copy.106
  391.7 4.1 fusion.93
  395.9 4.4 fusion.80
  400.6 6.4 copy.107
  407.0 4.7 fusion.78
  426.8 4.6 broadcast_select_fusion
  431.4 66.6 %reduce-scatter.19.cloned.1.call-done = bf16[256,64]{0,1:T(8,128)(2,1)} async-done(((bf16[256,1024]{0,1:T(8,128)(2,1)}), bf16[256,64]{0,1:T(8,128)(2,1)}) %reduce-scatter.19.cloned.1.call-update) | async-done | bytes 32784 | tf_op jit(solution)/shard_map/reduce_scatter | solution.py:164
  505.9 5.6 convolution_convert_fusion.2
  511.6 5.4 convolution_convert_fusion.3
  517.0 72.8 %all-reduce.1 = bf16[256,16]{1,0:T(8,128)(2,1)S(1)} all-reduce(bf16[256,16]{1,0:T(8,128)(2,1)S(1)} %get-tuple-element.90), channel_id=5, replica_groups=mesh['section'=2,'dp'=4,'mp'=16] {'mp'}, use_global_device_ids=true, to_apply=%region_19.20.clone | all-reduce | flops 4096 | bytes 16384
  592.8 16.7 %reduce-scatter.23.cloned.1.call-done = bf16[2048,32]{0,1:T(8,128)(2,1)} async-done(((bf16[8192,32]{0,1:T(8,128)(2,1)}), bf16[2048,32]{0,1:T(8,128)(2,1)}) %reduce-scatter.23.cloned.1.call-update) | async-done | bytes 131088 | tf_op jit(solution)/shard_map/reduce_scatter | solution.py:283
  609.5 31.4 %reduce-scatter.21.cloned.1.call-done = bf16[2048,32]{0,1:T(8,128)(2,1)} async-done(((bf16[8192,32]{0,1:T(8,128)(2,1)}), bf16[2048,32]{0,1:T(8,128)(2,1)}) %reduce-scatter.21.cloned.1.call-update) | async-done | bytes 131088 | tf_op jit(solution)/shard_map/reduce_scatter | solution.py:280
  640.9 54.1 %reduce-scatter.25.cloned.1.call-done = bf16[2048,256]{1,0:T(8,128)(2,1)} async-done(((bf16[8192,256]{1,0:T(8,128)(2,1)}), bf16[2048,256]{1,0:T(8,128)(2,1)}) %reduce-scatter.25.cloned.1.call-update) | async-done | bytes 1048592 | tf_op jit(solution)/shard_map/reduce_scatter | solution.py:286
  694.9 54.3 %reduce-scatter.15.cloned.1.call-done = bf16[2048,256]{1,0:T(8,128)(2,1)} async-done(((bf16[8192,256]{1,0:T(8,128)(2,1)}), bf16[2048,256]{1,0:T(8,128)(2,1)}) %reduce-scatter.15.cloned.1.call-update) | async-done | bytes 1048592 | tf_op jit(solution)/shard_map/reduce_scatter | solution.py:277
  (113 shorter events, 51.2 us)
Async XLA Ops:
  7.2 33.4 %copy-start.21 = (s32[1,4]{1,0:T(1,128)S(1)}, s32[1,4]{1,0:T(1,128)}, u32[]{:S(2)}) copy-start(s32[1,4]{1,0:T(1,128)} %param.16) | copy-start | bytes 52
  7.2 33.5 %copy-start.14 = (bf16[1,8192]{1,0:T(2,128)(2,1)S(1)}, bf16[1,8192]{1,0:T(2,128)(2,1)}, u32[]{:S(2)}) copy-start(bf16[1,8192]{1,0:T(2,128)(2,1)} %param.17) | copy-start | bytes 49156
  7.2 215.1 %reduce-scatter.11.cloned.1.call-start = ((), (), s32[]{:S(2)}) async-start(), calls=%async_computation.8 | async-start | bytes 4456448 | tf_op jit(solution)/shard_map/reduce_scatter | solution.py:158
  9.4 25.3 %collective-permute-start = (bf16[2,8192,32]{1,2,0:T(8,128)(2,1)S(1)}, bf16[2,8192,32]{1,2,0:T(8,128)(2,1)}, u32[]{:S(2)}, u32[]{:S(2)}) collective-permute-start(bf16[2,8192,32]{1,2,0:T(8,128)(2,1)S(1)} %constant_dynamic-update-slice_fusion), channel_id=1, source_target_pairs={{0,1},{1,0},{2,3},{3,2},{4,5},{5,4},{6,7},{7,6},{8,9},{9,8},{10,11... | collective-permute-start | bytes 3145736 | tf_op jit(solution)/shard_map/ppermute | solution.py:20
  36.8 48.6 %collective-permute-start.1 = (bf16[2,8192,64]{1,2,0:T(8,128)(2,1)S(1)}, bf16[2,8192,64]{1,2,0:T(8,128)(2,1)}, u32[]{:S(2)}, u32[]{:S(2)}) collective-permute-start(bf16[2,8192,64]{1,2,0:T(8,128)(2,1)S(1)} %maximum_select_fusion.1), channel_id=1, source_target_pairs={{0,2},{1,3},{2,0},{3,1},{4,6},{5,7},{6,4},{7,5},{8,10},{9,11},{10,... | collective-permute-start | bytes 6291464 | tf_op jit(solution)/shard_map/ppermute | solution.py:20
  99.6 183.8 %copy-start.8 = (bf16[256,1024]{0,1:T(8,128)(2,1)}, bf16[256,1024]{0,1:T(8,128)(2,1)S(1)}, u32[]{:S(2)}) copy-start(bf16[256,1024]{0,1:T(8,128)(2,1)S(1)} %get-tuple-element.95) | copy-start | bytes 1572868
  99.7 182.4 %all-gather.2.cloned.1.call-start = ((), (), s32[]{:S(2)}) async-start(), calls=%async_computation.9 | async-start | bytes 4456448 | tf_op jit(solution)/shard_map/all_gather | solution.py:175
  224.3 207.1 %reduce-scatter.17.cloned.1.call-start = ((), (), s32[]{:S(2)}) async-start(), calls=%async_computation.12 | async-start | bytes 557056 | tf_op jit(solution)/shard_map/reduce_scatter | solution.py:164
  282.1 93.6 %collective-permute-start.2 = (bf16[256,8192]{1,0:T(8,128)(2,1)}, bf16[256,8192]{1,0:T(8,128)(2,1)}, u32[]{:S(2)}, u32[]{:S(2)}) collective-permute-start(bf16[256,8192]{1,0:T(8,128)(2,1)} %all-gather.2.cloned.1.call-done), channel_id=1, source_target_pairs={{64,0},{65,1},{66,2},{67,3},{68,4},{69,5},{70,6},{71,7},{72,8},{73... | collective-permute-start | bytes 12582920 | tf_op jit(solution)/shard_map/ppermute | solution.py:16
  283.4 214.6 %reduce-scatter.19.cloned.1.call-start = ((), (), s32[]{:S(2)}) async-start(), calls=%async_computation.13 | async-start | bytes 557056 | tf_op jit(solution)/shard_map/reduce_scatter | solution.py:164
  375.8 5.3 copy-start.2
  382.0 3.2 copy-start.19
  414.8 4.5 copy-start.12
  415.6 3.7 copy-start.6
  421.5 3.6 copy-start.13
  421.5 3.6 copy-start.20
  426.2 164.4 %reduce-scatter.13.cloned.1.call-start = ((), (), s32[]{:S(2)}) async-start(), calls=%async_computation.10 | async-start | bytes 4456448 | tf_op jit(solution)/shard_map/reduce_scatter | solution.py:158
  426.8 182.7 %reduce-scatter.23.cloned.1.call-start = ((), (), s32[]{:S(2)}) async-start(), calls=%async_computation.15 | async-start | bytes 655360 | tf_op jit(solution)/shard_map/reduce_scatter | solution.py:283
  431.4 70.5 %copy-start.15 = (bf16[256,64]{0,1:T(8,128)(2,1)S(1)}, bf16[256,64]{0,1:T(8,128)(2,1)}, u32[]{:S(2)}) copy-start(bf16[256,64]{0,1:T(8,128)(2,1)} %reduce-scatter.17.cloned.1.call-done) | copy-start | bytes 98308
  498.1 3.9 copy-start.16
  501.9 138.9 %reduce-scatter.21.cloned.1.call-start = ((), (), s32[]{:S(2)}) async-start(), calls=%async_computation.14 | async-start | bytes 655360 | tf_op jit(solution)/shard_map/reduce_scatter | solution.py:280
  505.9 189.1 %reduce-scatter.25.cloned.1.call-start = ((), (), s32[]{:S(2)}) async-start(), calls=%async_computation.16 | async-start | bytes 5242880 | tf_op jit(solution)/shard_map/reduce_scatter | solution.py:286
  511.5 237.7 %reduce-scatter.15.cloned.1.call-start = ((), (), s32[]{:S(2)}) async-start(), calls=%async_computation.11 | async-start | bytes 5242880 | tf_op jit(solution)/shard_map/reduce_scatter | solution.py:277
  517.0 73.7 %copy-start.7 = (bf16[256,512]{1,0:T(8,128)(2,1)S(1)}, bf16[256,512]{1,0:T(8,128)(2,1)}, u32[]{:S(2)}) copy-start(bf16[256,512]{1,0:T(8,128)(2,1)} %subtract_convert_fusion.1) | copy-start | bytes 786436
  (3 other events, 3.7 us)
Sparse Core Ops, SparseCore 0:
  99.8 122.4 reduce-scatter.10
  225.2 56.8 all-gather.1
  286.2 72.1 reduce-scatter.16
  426.3 71.6 reduce-scatter.18
  501.6 76.9 reduce-scatter.12
  581.6 27.7 reduce-scatter.22
  612.8 27.9 reduce-scatter.20
  644.1 50.8 reduce-scatter.24
  698.3 50.8 reduce-scatter.14
where the time goes:
time: 763 us; the launch traced here: 756 us
  waiting for transfers between devices  486 us (64%)
  blocking collectives  148 us (19%)
  matrix products  48.1 us (6%)
  local copies, waits for them, and re-layouts  24.4 us (3%)
  other arithmetic  22.2 us (3%)
  between operations  14.3 us (2%)
    unnamed x2, blocking collectives  148 us
    ppermute x1, waiting for transfers between devices, passed_along(): return lax.ppermute(shard, axis, pairs)  92.3 us
    ppermute x2, waiting for transfers between devices, swapped(): lax.ppermute(shard, axis, [(i, i ^ 1 << stride) for i in range(lax.axis_s...  67.3 us
    reduce_scatter x2, waiting for transfers between devices, reduce_heads(): lax.psum_scatter(key_value.astype(jnp.bfloat16), 'mp', scatter_dimension=...  66.6 us
    all_gather x1, waiting for transfers between devices, collect(): return lax.all_gather(values, 'mp', axis=1, tiled=True)  57.7 us
    reduce_scatter x1, waiting for transfers between devices, on_device(): lax.psum_scatter(part_q.astype(jnp.bfloat16), 'dp', scatter_dimension=0,...  54.3 us
    reduce_scatter x1, waiting for transfers between devices, on_device(): lax.psum_scatter(part_o.astype(jnp.bfloat16), 'dp', scatter_dimension=0,...  54.1 us
    reduce_scatter x2, waiting for transfers between devices, reduce_heads(): lax.psum_scatter(grad_normed.astype(jnp.bfloat16), 'mp', scatter_dimensio...  45.1 us
  transfers between devices with their start and end apart: 12, of which 10 were waited for; matrix products, arithmetic and copies ran while one was open for 10% of the time, Pallas kernels for 0%

commit v1 on v0

v1 whole, which is shorter than its diff:
```python
import functools
import math

import jax
import jax.numpy as jnp
import numpy as np
from jax import lax
from jax.experimental import pallas as pl
from jax.experimental.pallas import tpu as pltpu
from jax.sharding import PartitionSpec as P

HD = 128
SEQ = 256
D = 8192
TILE = 512
BLOCK = 2048
KV = 64
ROWS = 320
CHUNK = 1024
N_CHUNK = D // CHUNK
SCALE = 1.0 / math.sqrt(HD)
F32 = jnp.float32
BF16 = jnp.bfloat16
MESH = pl.DeviceIdType.MESH


def dot_nn(a, b):
    return lax.dot_general(a, b, (((1,), (0,)), ((), ())), preferred_element_type=F32)


def dot_nt(a, b):
    return lax.dot_general(a, b, (((1,), (1,)), ((), ())), preferred_element_type=F32)


def ring(v):
    return lax.rem(v + 4, 4)


def begin_of(lens, places):
    start = jnp.int32(0)
    begins = jnp.zeros_like(places)
    for i in range(4):
        begins = jnp.maximum(begins, jnp.where(places >= start, start, 0))
        start = start + lens[0, i]
    return begins


def swap_rows(v):
    return jnp.concatenate([v[64:128], v[0:64]], axis=0)


def relay_kernel(
    late, cot, early, lens, gain, w_q, w_k, w_v, w_o, freq,
    gin, tok_g, up_g, d_g, c_g,
    tok, wq, wkv, wo, up, part,
    xq, xkv, dctx, probs, qs, kv_all, kvp_send, kvp_recv, cosv, sinv, inv_ref, cs_ref,
    aq, akv, dqkv, ctx,
    rrel, racc, rdir, summed, rrel2, racc2, rdir2,
    load_sem, up_sem, loc_sem, send_sem, recv_sem,
):
    s = lax.axis_index("section")
    d = lax.axis_index("dp")
    m = lax.axis_index("mp")
    y, z = lax.div(m, 4), lax.rem(m, 4)
    h, c = lax.div(d, 2), lax.rem(d, 2)
    d_of = [d, h * 2 + (1 - c), (1 - h) * 2 + c, (1 - h) * 2 + (1 - c)]
    is_later = s == 1
    is_earlier = s == 0

    def mp_id(yy, zz):
        return {"mp": yy * 4 + zz}

    z_peer = [mp_id(y, ring(z + o)) for o in range(4)]
    y_right, y_left = mp_id(ring(y + 1), z), mp_id(ring(y - 1), z)
    z_right, z_left = z_peer[1], z_peer[3]
    dp_peer = [{"dp": d_of[o]} for o in range(4)]
    cross_peer = [None, None] + [{"section": 1 - s, "dp": d_of[o]} for o in (2, 3)]
    hand_peer = {"section": 1 - s}

    def tok_copy(source, i):
        return pltpu.make_async_copy(
            source.at[:, pl.ds(i * CHUNK, CHUNK)], tok.at[:, pl.ds(i * CHUNK, CHUNK)], load_sem.at[0, i]
        )

    def wq_copy(i):
        return pltpu.make_async_copy(
            w_q.at[pl.ds(i * CHUNK, CHUNK), :], wq.at[pl.ds(i * CHUNK, CHUNK), :], load_sem.at[1, i]
        )

    def wk_copy(i):
        return pltpu.make_async_copy(
            w_k.at[:, pl.ds(i * CHUNK, CHUNK)], wkv.at[0:32, pl.ds(i * CHUNK, CHUNK)], load_sem.at[2, i]
        )

    def wv_copy(i):
        return pltpu.make_async_copy(
            w_v.at[:, pl.ds(i * CHUNK, CHUNK)], wkv.at[32:64, pl.ds(i * CHUNK, CHUNK)], load_sem.at[3, i]
        )

    def wo_copy(i):
        return pltpu.make_async_copy(
            w_o.at[pl.ds(i * CHUNK, CHUNK), :], wo.at[pl.ds(i * CHUNK, CHUNK), :], load_sem.at[4, i]
        )

    def cot_copy(yy, zz):
        return pltpu.make_async_copy(
            cot.at[:, pl.ds(pl.multiple_of((yy * 4 + zz) * TILE, TILE), TILE)], up.at[yy, zz], up_sem.at[yy, zz]
        )

    def per_section(later, earlier):
        pl.when(is_later)(later)
        pl.when(is_earlier)(earlier)

    for i in range(N_CHUNK):
        per_section(lambda: tok_copy(late, i).start(), lambda: tok_copy(early, i).start())
        wq_copy(i).start()
        wk_copy(i).start()
        wv_copy(i).start()
    for i in range(N_CHUNK):
        wo_copy(i).start()

    @pl.when(is_later)
    def _():
        for yy in range(4):
            for zz in range(4):
                cot_copy(yy, zz).start()

    barrier = pltpu.get_barrier_semaphore()
    greeted = [z_peer[1], z_peer[2], z_peer[3], y_right, y_left, hand_peer]
    greeted += dp_peer[1:] + cross_peer[2:]
    for peer in greeted:
        pl.semaphore_signal(barrier, inc=1, device_id=peer, device_id_type=MESH)
    pl.semaphore_wait(barrier, len(greeted))

    count = [0]

    def slot():
        count[0] += 1
        return count[0] - 1

    def remote(src, dst, n, peer):
        return pltpu.make_async_remote_copy(
            src_ref=src, dst_ref=dst, send_sem=send_sem.at[n], recv_sem=recv_sem.at[n],
            device_id=peer, device_id_type=MESH,
        )

    def cols(index):
        return pl.ds(pl.multiple_of(index * BLOCK, BLOCK), BLOCK)

    tok_slots = [None] + [slot() for _ in range(3)]
    up_slots = [None] + [slot() for _ in range(3)]

    def tok_send(source, o):
        peer = dp_peer[1] if o == 1 else cross_peer[o]
        return remote(source.at[:, cols(d_of[o])], tok_g.at[d], tok_slots[o], peer)

    def cot_send(o):
        peer = dp_peer[1] if o == 1 else cross_peer[o]
        return remote(cot.at[:, cols(d_of[o])], up_g.at[d], up_slots[o], peer)

    def tok_keep(source):
        return pltpu.make_async_copy(source.at[:, cols(d)], tok_g.at[d], loc_sem.at[0])

    def cot_keep():
        return pltpu.make_async_copy(cot.at[:, cols(d)], up_g.at[d], loc_sem.at[1])

    def later_starts():
        tok_send(late, 1).start()
        tok_send(early, 2).start()
        tok_send(early, 3).start()
        cot_send(1).start()
        tok_keep(late).start()
        cot_keep().start()

    def earlier_starts():
        tok_send(early, 1).start()
        tok_send(late, 2).start()
        tok_send(late, 3).start()
        cot_send(2).start()
        cot_send(3).start()
        tok_keep(early).start()

    per_section(later_starts, earlier_starts)

    lane = lax.broadcasted_iota(jnp.int32, (SEQ, HD), 1)
    place = lax.broadcasted_iota(jnp.int32, (SEQ, HD), 0)
    offset = (place - begin_of(lens, place)).astype(F32)
    angle = offset * freq[0:1, :]
    cosv[...] = jnp.cos(angle)
    sinv[...] = jnp.where(lane < 64, -1.0, 1.0) * jnp.sin(angle)

    xq[...] = jnp.zeros_like(xq)
    xkv[...] = jnp.zeros_like(xkv)
    inv_ref[...] = jnp.zeros_like(inv_ref)

    def project(i, carry):
        span = pl.ds(pl.multiple_of(i * CHUNK, CHUNK), CHUNK)
        tok_copy(late, i).wait()
        wq_copy(i).wait()
        wk_copy(i).wait()
        wv_copy(i).wait()
        t = tok[:, span].astype(F32)
        x = (t * gain[0:1, span].astype(F32)).astype(BF16)
        inv_ref[...] += jnp.sum(t * t, axis=1, keepdims=True)
        xq[...] += dot_nn(x, wq[span, :])
        xkv[...] += dot_nt(x, wkv[:, span])
        return carry

    lax.fori_loop(0, N_CHUNK, project, 0)
    inv_ref[...] = lax.rsqrt(inv_ref[...] * (1.0 / D) + 1e-5)
    inv = inv_ref[:, 0:1]

    kv_all[z] = jnp.transpose(xkv[...] * inv).astype(BF16)
    kv_slots = [None] + [slot() for _ in range(3)]
    kv_copies = [remote(kv_all.at[z], kv_all.at[z], kv_slots[o], z_peer[o]) for o in (1, 2, 3)]
    for copy in kv_copies:
        copy.start()

    cos = cosv[...]
    sin = sinv[...]
    cos_t = jnp.transpose(cos)
    sin_t = jnp.transpose(sin)
    for j in range(2):
        q = xq[:, j * HD:(j + 1) * HD] * inv
        qs[j] = (q * cos + pltpu.roll(q, 64, 1) * sin).astype(BF16)
    for copy in kv_copies:
        copy.wait_recv()
    k = jnp.concatenate([kv_all[i, 0:32] for i in range(4)], axis=0).astype(F32)
    k_t = (k * cos_t + swap_rows(k) * sin_t).astype(BF16)
    v_t = jnp.concatenate([kv_all[i, 32:64] for i in range(4)], axis=0)

    row = lax.broadcasted_iota(jnp.int32, (SEQ, SEQ), 0)
    col = lax.broadcasted_iota(jnp.int32, (SEQ, SEQ), 1)
    allowed = (begin_of(lens, row) == begin_of(lens, col)) & (col <= row)
    for j in range(2):
        scores = jnp.where(allowed, dot_nn(qs[j], k_t) * SCALE, -1e30)
        peak = jnp.max(scores, axis=1, keepdims=True)
        ex = jnp.exp(scores - peak)
        pr = ex / jnp.sum(ex, axis=1, keepdims=True)
        probs[j] = pr
        ctx[j * HD:(j + 1) * HD, :] = dot_nt(v_t, pr.astype(BF16)).astype(BF16)
    ctx_slots = [None] + [slot() for _ in range(3)]
    ctx_copies = [remote(ctx, c_g.at[d], ctx_slots[o], dp_peer[o]) for o in (1, 2, 3)]
    ctx_keep = pltpu.make_async_copy(ctx, c_g.at[d], loc_sem.at[2])
    for copy in ctx_copies:
        copy.start()
    ctx_keep.start()

    for i in range(N_CHUNK):
        wo_copy(i).wait()
    dctx[...] = jnp.zeros_like(dctx)

    def wo_rows(yy, zz):
        return pl.ds(pl.multiple_of((yy * 4 + zz) * TILE, TILE), TILE)

    def halves(k):
        return pl.ds(k * 128, 128)

    def add_context(k, yy, zz):
        dctx[halves(k), :] += dot_nn(up[yy, zz, halves(k), :], wo[wo_rows(yy, zz), :])

    own_slots = [slot() for _ in range(2)]
    p1_slots = [[slot() for _ in range(4)] for _ in range(2)]
    p2_slots = [[[slot() for _ in range(4)] for _ in range(4)] for _ in range(2)]

    def hand_copy(k):
        return remote(up.at[y, z, halves(k), :], up.at[y, z, halves(k), :], own_slots[k], hand_peer)

    def at(k, first, second):
        return (second, first) if k == 0 else (first, second)

    @pl.when(is_later)
    def _():
        def body(i, carry):
            yy, zz = lax.div(i, 4), lax.rem(i, 4)
            cot_copy(yy, zz).wait()
            dctx[...] += dot_nn(up[yy, zz], wo[wo_rows(yy, zz), :])
            return carry

        lax.fori_loop(0, 16, body, 0)

    @pl.when(is_earlier)
    def _():
        first_of, second_of = (z, y), (y, z)
        first_right, first_left = (z_right, y_right), (z_left, y_left)
        second_right, second_left = (y_right, z_right), (y_left, z_left)
        pending = []

        def piece(k, a, b, lo, n):
            yy, zz = at(k, a, b)
            return up.at[yy, zz, pl.ds(k * 128 + lo, n), :]

        def send(k, a, b, lo, n, index, peer):
            ref = piece(k, a, b, lo, n)
            copy = remote(ref, ref, index, peer)
            copy.start()
            pending.append(copy)

        def arrived(k, a, b, lo, n, index):
            ref = piece(k, a, b, lo, n)
            remote(ref, ref, index, hand_peer).wait_recv()

        def spread(k, o):
            a = ring(first_of[k] + o)
            send(k, a, second_of[k], 0, 128, p2_slots[k][o][0], second_right[k])
            send(k, a, second_of[k], 0, 128, p2_slots[k][o][1], second_left[k])

        for k in range(2):
            hand_copy(k).wait_recv()
            send(k, first_of[k], second_of[k], 0, 128, p1_slots[k][0], first_right[k])
            send(k, first_of[k], second_of[k], 0, 128, p1_slots[k][1], first_left[k])
            spread(k, 0)
        for k in range(2):
            add_context(k, y, z)
        for k in range(2):
            a, b = ring(first_of[k] - 1), second_of[k]
            arrived(k, a, b, 0, 128, p1_slots[k][0])
            send(k, a, b, 0, 64, p1_slots[k][2], first_right[k])
            spread(k, 3)
            a = ring(first_of[k] + 1)
            arrived(k, a, b, 0, 128, p1_slots[k][1])
            send(k, a, b, 64, 64, p1_slots[k][3], first_left[k])
            spread(k, 1)
        for k in range(2):
            for o in (3, 1):
                add_context(k, *at(k, ring(first_of[k] + o), second_of[k]))

        def relay(k, o):
            a = ring(first_of[k] + o)
            left, right = ring(second_of[k] - 1), ring(second_of[k] + 1)
            arrived(k, a, left, 0, 128, p2_slots[k][o][0])
            send(k, a, left, 0, 64, p2_slots[k][o][2], second_right[k])
            arrived(k, a, right, 0, 128, p2_slots[k][o][1])
            send(k, a, right, 64, 64, p2_slots[k][o][3], second_left[k])
            add_context(k, *at(k, a, left))
            add_context(k, *at(k, a, right))

        for k in range(2):
            relay(k, 0)
        for k in range(2):
            a, b = ring(first_of[k] + 2), second_of[k]
            arrived(k, a, b, 0, 64, p1_slots[k][2])
            arrived(k, a, b, 64, 64, p1_slots[k][3])
            spread(k, 2)
            add_context(k, *at(k, a, b))
        for o in (3, 1, 2):
            for k in range(2):
                relay(k, o)
        for o in (0, 3, 1, 2):
            for k in range(2):
                a, b = ring(first_of[k] + o), ring(second_of[k] + 2)
                arrived(k, a, b, 0, 64, p2_slots[k][o][2])
                arrived(k, a, b, 64, 64, p2_slots[k][o][3])
                add_context(k, *at(k, a, b))
        for copy in pending:
            copy.wait_send()
        for o in (2, 3, 1):
            for zz in range(4):
                remote(
                    up.at[d_of[o], zz], up_g.at[d, :, pl.ds(zz * TILE, TILE)], up_slots[o], dp_peer[o]
                ).start()
        for zz in range(4):
            pltpu.make_async_copy(up.at[d, zz], up_g.at[d, :, pl.ds(zz * TILE, TILE)], loc_sem.at[1]).start()

    dk_t = jnp.zeros((HD, SEQ), F32)
    dv_t = jnp.zeros((HD, SEQ), F32)
    dq_list = []
    for j in range(2):
        grad = dctx[:, j * HD:(j + 1) * HD]
        grad_low = grad.astype(BF16)
        pr = probs[j]
        dp = dot_nn(grad_low, v_t)
        ds = (pr * (dp - jnp.sum(dp * pr, axis=1, keepdims=True)) * SCALE).astype(BF16)
        dq = dot_nt(k_t, ds)
        dq_list.append(dq * cos_t - swap_rows(dq) * sin_t)
        dk_t += dot_nn(jnp.transpose(qs[j].astype(F32)).astype(BF16), ds)
        dv_t += dot_nn(jnp.transpose(grad).astype(BF16), pr.astype(BF16))
    dk_t = dk_t * cos_t - swap_rows(dk_t) * sin_t
    for i in range(4):
        kvp_send[i, 0:32] = dk_t[i * 32:(i + 1) * 32].astype(BF16)
        kvp_send[i, 32:64] = dv_t[i * 32:(i + 1) * 32].astype(BF16)
    kvp_slots = [None] + [slot() for _ in range(3)]
    kvp_copies = [
        remote(kvp_send.at[ring(z + o)], kvp_recv.at[o], kvp_slots[o], z_peer[o]) for o in (1, 2, 3)
    ]
    for copy in kvp_copies:
        copy.start()
    inv_t = jnp.transpose(inv_ref[...])[0:1, :]
    dq_t = jnp.concatenate(dq_list, axis=0)
    dqkv[0:256, :] = (dq_t * inv_t).astype(BF16)
    dq = jnp.transpose(dq_t)
    aq[...] = (dq * inv).astype(BF16)
    stat = jnp.sum(dq * xq[...], axis=1, keepdims=True)
    for copy in kvp_copies:
        copy.wait_recv()
    dkv_t = kvp_send[z].astype(F32)
    for o in (1, 2, 3):
        dkv_t += kvp_recv[o].astype(F32)
    dqkv[256:320, :] = (dkv_t * inv_t).astype(BF16)
    dkv = jnp.transpose(dkv_t)
    akv[...] = (dkv * inv).astype(BF16)
    stat += jnp.sum(dkv * xkv[...], axis=1, keepdims=True)
    cs_ref[...] = jnp.broadcast_to(inv * inv * inv * stat * (1.0 / D), cs_ref.shape)
    d_slots = [None] + [slot() for _ in range(3)]
    d_copies = [remote(dqkv, d_g.at[d], d_slots[o], dp_peer[o]) for o in (1, 2, 3)]
    d_keep = pltpu.make_async_copy(dqkv, d_g.at[d], loc_sem.at[3])
    for copy in d_copies:
        copy.start()
    d_keep.start()

    ring_of, other_of = (y, z), (z, y)
    right_1, left_1 = (y_right, z_right), (y_left, z_left)
    right_2, left_2 = (z_right, y_right), (z_left, y_left)

    def block(k, a, lo, n):
        if k == 0:
            return part.at[a, pl.ds(lo, n), halves(k), :]
        return part.at[pl.ds(lo, n), a, halves(k), :]

    def tile(k, a, b):
        return (a, b) if k == 0 else (b, a)

    def compute(k, a):
        def body(b, carry):
            yy, zz = tile(k, a, b)
            span = wo_rows(yy, zz)
            total = dot_nt(aq[halves(k), :], wq[span, :]) + dot_nn(akv[halves(k), :], wkv[:, span])
            total = total * gain[0:1, span].astype(F32) - tok[halves(k), span].astype(F32) * cs_ref[halves(k), 0:1]
            part[yy, zz, halves(k), :] = total.astype(BF16)
            return carry

        lax.fori_loop(0, 4, body, 0)

    rs1 = [[slot() for _ in range(6)] for _ in range(2)]
    rs2 = [[slot() for _ in range(6)] for _ in range(2)]
    sent = []

    def go(src, dst, n, peer):
        copy = remote(src, dst, n, peer)
        copy.start()
        sent.append(copy)

    for k in range(2):
        i = ring_of[k]
        compute(k, ring(i + 2))
        go(block(k, ring(i + 2), 0, 2), rrel.at[k, 0:2], rs1[k][0], right_1[k])
        go(block(k, ring(i + 2), 2, 2), rrel.at[k, 2:4], rs1[k][1], left_1[k])
    for k in range(2):
        i = ring_of[k]
        compute(k, ring(i + 1))
        go(block(k, ring(i + 1), 2, 2), rdir.at[k, 2:4], rs1[k][5], right_1[k])
        compute(k, ring(i - 1))
        go(block(k, ring(i - 1), 0, 2), rdir.at[k, 0:2], rs1[k][4], left_1[k])
    for k in range(2):
        compute(k, ring_of[k])

    def landed(ref, n):
        remote(ref, ref, n, y_right).wait_recv()

    for k in range(2):
        i = ring_of[k]
        landed(rrel.at[k, 0:2], rs1[k][0])
        for b in range(2):
            yy, zz = tile(k, ring(i + 1), b)
            part[yy, zz, halves(k), :] = (
                part[yy, zz, halves(k), :].astype(F32) + rrel[k, b].astype(F32)
            ).astype(BF16)
        go(block(k, ring(i + 1), 0, 2), racc.at[k, 0:2], rs1[k][2], right_1[k])
        landed(rrel.at[k, 2:4], rs1[k][1])
        for b in range(2, 4):
            yy, zz = tile(k, ring(i - 1), b)
            part[yy, zz, halves(k), :] = (
                part[yy, zz, halves(k), :].astype(F32) + rrel[k, b].astype(F32)
            ).astype(BF16)
        go(block(k, ring(i - 1), 2, 2), racc.at[k, 2:4], rs1[k][3], left_1[k])

    def collect(k, b):
        yy, zz = tile(k, ring_of[k], b)
        summed[k, b] = (
            part[yy, zz, halves(k), :].astype(F32) + racc[k, b].astype(F32) + rdir[k, b].astype(F32)
        ).astype(BF16)

    for k in range(2):
        j = other_of[k]
        landed(rdir.at[k, 0:2], rs1[k][4])
        landed(rdir.at[k, 2:4], rs1[k][5])
        landed(racc.at[k, 0:2], rs1[k][2])
        landed(racc.at[k, 2:4], rs1[k][3])
        collect(k, ring(j + 2))
        go(summed.at[k, ring(j + 2), 0:64], rrel2.at[k, 0:64], rs2[k][0], right_2[k])
        go(summed.at[k, ring(j + 2), 64:128], rrel2.at[k, 64:128], rs2[k][1], left_2[k])
        collect(k, ring(j + 1))
        go(summed.at[k, ring(j + 1), 64:128], rdir2.at[k, 64:128], rs2[k][5], right_2[k])
        collect(k, ring(j - 1))
        go(summed.at[k, ring(j - 1), 0:64], rdir2.at[k, 0:64], rs2[k][4], left_2[k])
        collect(k, j)
    for k in range(2):
        j = other_of[k]
        landed(rrel2.at[k, 0:64], rs2[k][0])
        a = ring(j + 1)
        summed[k, a, 0:64] = (summed[k, a, 0:64].astype(F32) + rrel2[k, 0:64].astype(F32)).astype(BF16)
        go(summed.at[k, a, 0:64], racc2.at[k, 0:64], rs2[k][2], right_2[k])
        landed(rrel2.at[k, 64:128], rs2[k][1])
        a = ring(j - 1)
        summed[k, a, 64:128] = (summed[k, a, 64:128].astype(F32) + rrel2[k, 64:128].astype(F32)).astype(BF16)
        go(summed.at[k, a, 64:128], racc2.at[k, 64:128], rs2[k][3], left_2[k])
    for k in range(2):
        j = other_of[k]
        landed(rdir2.at[k, 0:64], rs2[k][4])
        landed(rdir2.at[k, 64:128], rs2[k][5])
        landed(racc2.at[k, 0:64], rs2[k][2])
        landed(racc2.at[k, 64:128], rs2[k][3])
        gin[halves(k), :] = (
            up[y, z, halves(k), :].astype(F32)
            + summed[k, j].astype(F32)
            + racc2[k].astype(F32)
            + rdir2[k].astype(F32)
        ).astype(BF16)

        @pl.when(is_later)
        def _():
            remote(gin.at[halves(k), :], up.at[y, z, halves(k), :], own_slots[k], hand_peer).start()

    for copy in sent + kv_copies + ctx_copies + kvp_copies + d_copies:
        copy.wait_send()
    for copy in ctx_copies + d_copies:
        copy.wait_recv()
    ctx_keep.wait()
    d_keep.wait()

    @pl.when(is_later)
    def _():
        for k in range(2):
            hand_copy(k).wait_send()

    tok_keep(late).wait()
    cot_keep().wait()
    for o in (1, 2, 3):
        copy = tok_send(late, o)
        copy.wait_send()
        copy.wait_recv()
        copy = cot_send(o)
        copy.wait_recv()

    @pl.when(is_later)
    def _():
        cot_send(1).wait_send()

    @pl.when(is_earlier)
    def _():
        for o in (1, 2, 3):
            cot_send(o).wait_send()
        for o in (2, 3):
            cot_send(o).wait_send()


N_SLOTS = 6 + 3 + 3 + 2 + 8 + 32 + 3 + 3 + 24


def relay(late, cot, early, lens, gain, w_q, w_k, w_v, w_o, freq):
    any_spec = pl.BlockSpec(memory_space=pl.ANY)
    vmem = pl.BlockSpec(memory_space=pltpu.VMEM)
    smem = pl.BlockSpec(memory_space=pltpu.SMEM)
    out_shape = (
        jax.ShapeDtypeStruct((SEQ, TILE), BF16),
        jax.ShapeDtypeStruct((4, SEQ, BLOCK), BF16),
        jax.ShapeDtypeStruct((4, SEQ, BLOCK), BF16),
        jax.ShapeDtypeStruct((4, ROWS, SEQ), BF16),
        jax.ShapeDtypeStruct((4, SEQ, SEQ), BF16),
    )
    scratch = [
        pltpu.VMEM((SEQ, D), BF16),
        pltpu.VMEM((D, 256), BF16),
        pltpu.VMEM((KV, D), BF16),
        pltpu.VMEM((D, 256), BF16),
        pltpu.VMEM((4, 4, SEQ, TILE), BF16),
        pltpu.VMEM((4, 4, SEQ, TILE), BF16),
        pltpu.VMEM((SEQ, 256), F32),
        pltpu.VMEM((SEQ, KV), F32),
        pltpu.VMEM((SEQ, 256), F32),
        pltpu.VMEM((2, SEQ, SEQ), F32),
        pltpu.VMEM((2, SEQ, HD), BF16),
        pltpu.VMEM((4, KV, SEQ), BF16),
        pltpu.VMEM((4, KV, SEQ), BF16),
        pltpu.VMEM((4, KV, SEQ), BF16),
        pltpu.VMEM((SEQ, HD), F32),
        pltpu.VMEM((SEQ, HD), F32),
        pltpu.VMEM((SEQ, HD), F32),
        pltpu.VMEM((SEQ, HD), F32),
        pltpu.VMEM((SEQ, 256), BF16),
        pltpu.VMEM((SEQ, KV), BF16),
        pltpu.VMEM((ROWS, SEQ), BF16),
        pltpu.VMEM((256, SEQ), BF16),
        pltpu.VMEM((2, 4, 128, TILE), BF16),
        pltpu.VMEM((2, 4, 128, TILE), BF16),
        pltpu.VMEM((2, 4, 128, TILE), BF16),
        pltpu.VMEM((2, 4, 128, TILE), BF16),
        pltpu.VMEM((2, 128, TILE), BF16),
        pltpu.VMEM((2, 128, TILE), BF16),
        pltpu.VMEM((2, 128, TILE), BF16),
        pltpu.SemaphoreType.DMA((5, N_CHUNK)),
        pltpu.SemaphoreType.DMA((4, 4)),
        pltpu.SemaphoreType.DMA((4,)),
        pltpu.SemaphoreType.DMA((N_SLOTS,)),
        pltpu.SemaphoreType.DMA((N_SLOTS,)),
    ]
    return pl.pallas_call(
        relay_kernel,
        out_shape=out_shape,
        in_specs=[any_spec, any_spec, any_spec, smem, vmem, any_spec, any_spec, any_spec, any_spec, vmem],
        out_specs=(vmem, any_spec, any_spec, any_spec, any_spec),
        scratch_shapes=scratch,
        compiler_params=pltpu.CompilerParams(
            collective_id=0, has_side_effects=True, vmem_limit_bytes=52 * 1024 * 1024
        ),
        name="relay",
    )(late, cot, early, lens, gain, w_q, w_k, w_v, w_o, freq)


def weights_kernel(tok, up, d_ref, c_ref, gain, gin, q_out, o_out, k_out, v_out, gin_out):
    i = pl.program_id(0)
    start = pl.multiple_of(lax.axis_index("dp") * BLOCK + i * TILE, TILE)
    total = dot_nn(d_ref[0], tok[0])
    for e in range(1, 4):
        total += dot_nn(d_ref[e], tok[e])
    total = total * gain[0:1, pl.ds(start, TILE)].astype(F32)
    q_out[...] = jnp.transpose(total[0:256]).astype(BF16)
    k_out[...] = total[256:288].astype(BF16)
    v_out[...] = total[288:320].astype(BF16)
    other = dot_nn(c_ref[0], up[0])
    for e in range(1, 4):
        other += dot_nn(c_ref[e], up[e])
    o_out[...] = jnp.transpose(other).astype(BF16)
    gin_out[...] = gin[...]


def weight_grads(tok_g, up_g, d_g, c_g, gain, gin):
    return pl.pallas_call(
        weights_kernel,
        grid=(4,),
        out_shape=(
            jax.ShapeDtypeStruct((BLOCK, 256), BF16),
            jax.ShapeDtypeStruct((BLOCK, 256), BF16),
            jax.ShapeDtypeStruct((32, BLOCK), BF16),
            jax.ShapeDtypeStruct((32, BLOCK), BF16),
            jax.ShapeDtypeStruct((SEQ, TILE), BF16),
        ),
        in_specs=[
            pl.BlockSpec((4, SEQ, TILE), lambda i: (0, 0, i)),
            pl.BlockSpec((4, SEQ, TILE), lambda i: (0, 0, i)),
            pl.BlockSpec((4, ROWS, SEQ), lambda i: (0, 0, 0)),
            pl.BlockSpec((4, SEQ, SEQ), lambda i: (0, 0, 0)),
            pl.BlockSpec((1, D), lambda i: (0, 0)),
            pl.BlockSpec((SEQ, TILE), lambda i: (0, 0)),
        ],
        out_specs=(
            pl.BlockSpec((TILE, 256), lambda i: (i, 0)),
            pl.BlockSpec((TILE, 256), lambda i: (i, 0)),
            pl.BlockSpec((32, TILE), lambda i: (0, i)),
            pl.BlockSpec((32, TILE), lambda i: (0, i)),
            pl.BlockSpec((SEQ, TILE), lambda i: (0, 0)),
        ),
        compiler_params=pltpu.CompilerParams(vmem_limit_bytes=40 * 1024 * 1024),
        name="weight_grads",
    )(tok_g, up_g, d_g, c_g, gain, gin)


def on_device(
    late_inputs, cotangent, early_inputs, doc_lengths, norm_gain, w_query, w_key, w_value, w_output
):
    half = 10000.0 ** (-np.arange(0, HD, 2).astype(np.float32) / HD)
    freq = jnp.asarray(np.concatenate([half, half]).astype(np.float32)[None, :])
    gin, tok_g, up_g, d_g, c_g = relay(
        late_inputs, cotangent, early_inputs, doc_lengths, norm_gain,
        w_query[0], w_key[0].T, w_value[0].T, w_output[0], freq,
    )
    grad_q, grad_o, grad_k, grad_v, grad_in = weight_grads(tok_g, up_g, d_g, c_g, norm_gain, gin)
    return grad_in[None], grad_q[None], grad_k.T[None], grad_v.T[None], grad_o[None]


def solution(mesh):
    in_specs = (
        P("dp", None),
        P("dp", None),
        P("dp", None),
        P("dp", None),
        P("section", None),
        P("section", None, "mp"),
        P("section", None, "mp"),
        P("section", None, "mp"),
        P("section", None, "mp"),
    )
    out_specs = (P("section", "dp", "mp"),) * 5
    return jax.shard_map(
        on_device, mesh=mesh, in_specs=in_specs, out_specs=out_specs, check_vma=False
    )
```

time: 763 us -> 148 us (0.19)
  waiting for transfers between devices: 486 us -> 0 us
  blocking collectives: 148 us -> 0 us
  Pallas kernels: 0 us -> 135 us
  matrix products: 48.1 us -> 0 us
  other arithmetic: 22.2 us -> 0 us
  local copies, waits for them, and re-layouts: 24.4 us -> 9.6 us
  between operations: 14.3 us -> 0.67 us
    reduce_scatter x8 -> x0, waiting for transfers between devices: 268 us -> none  [the longest x2 66.6 us: reduce_heads(): lax.psum_scatter(key_value.astype(jnp.bfloat16), 'mp', scatter_dimension=...]
    ppermute x3 -> x0, waiting for transfers between devices: 160 us -> none  [the longest x1 92.3 us: passed_along(): return lax.ppermute(shard, axis, pairs)]
    unnamed x2 -> x0, blocking collectives: 148 us -> none
    pallas_call x0 -> x2, Pallas kernels: none -> 135 us  [the longest x1 130 us: relay(): pl.pallas_call(relay_kernel, out_shape=out_shape, in_specs=[any_spec, any...]
    all_gather x1 -> x0, waiting for transfers between devices: 57.7 us -> none  [collect(): return lax.all_gather(values, 'mp', axis=1, tiled=True)]
    dot_general x16 -> x0, matrix products: 47.7 us -> none  [the longest x4 18.7 us: matmul_tn(): lax.dot_general(first_op, second_op, (((0,), (0,)), ((), ())), preferred_...]
    another operation x14 -> x0, local copies, waits for them, and re-layouts: 19 us -> none
    select_n x3 -> x0, other arithmetic: 11.2 us -> none  [the longest x2 6.63 us: on_device(): jnp.where(low_side, jnp.concatenate([joined, partner], axis=2), jnp.conca...]
  transfers between devices with their start and end apart: 12 -> 0, of which waited for: 10 -> 0; matrix products, arithmetic and copies ran while one was open for 10% -> 0% of each run, Pallas kernels for 0% -> 0%
where the time goes in v1:
time: 148 us; the launch traced here: 145 us
  Pallas kernels  135 us (91%)
  local copies, waits for them, and re-layouts  9.6 us (6%)
    pallas_call x1, Pallas kernels, relay(): pl.pallas_call(relay_kernel, out_shape=out_shape, in_specs=[any_spec, any...  130 us
    unnamed x16, local copies, waits for them, and re-layouts  9.6 us
    pallas_call x1, Pallas kernels, weight_grads(): pl.pallas_call(weights_kernel, grid=(4,), out_shape=(jax.ShapeDtypeStruct...  4.86 us

profile of v1, /device:TPU:0, one launch (start us, length us, event | category | flops | bytes accessed | tf_op | source)
XLA Modules:
  0.0 145.4 jit_solution(6420108294417159680)
XLA Ops:
  0.6 0.0 copy-start.3
  0.6 1.0 copy-done.3
  1.7 0.0 copy-start.4
  1.7 1.0 copy-done.4
  2.7 0.0 copy-start.5
  2.7 0.8 copy-done.5
  3.5 0.0 copy-start.6
  3.5 0.7 copy-done.6
  4.1 0.0 copy-start.7
  4.1 0.7 copy-done.7
  4.8 130.3 %relay.1 = (bf16[256,512]{1,0:T(8,128)(2,1)S(1)}, bf16[4,256,2048]{2,1,0:T(8,128)(2,1)}, bf16[4,256,2048]{2,1,0:T(8,128)(2,1)}, bf16[4,320,256]{2,1,0:T(8,128)(2,1)}, bf16[4,256,256]{2,1,0:T(8,128)(2,1)S(1)}) custom-call(bf16[256,8192]{1,0:T(8,128)(2,1)} %late.1, bf16[256,8192]{1,0:T(8,128)(2,1)} %cot.1, bf16[256,8192]{1,0:T(8,128)(2,1)} %early.1, ...), custom_call_target="tpu_custom_call" | custom-call | tf_op jit(solution)/shard_map/relay/pallas_call | solution.py:607
  135.1 0.0 copy-start
  135.1 2.2 %copy-done = bf16[4,256,2048]{2,1,0:T(8,128)(2,1)S(1)} copy-done((bf16[4,256,2048]{2,1,0:T(8,128)(2,1)S(1)}, bf16[4,256,2048]{2,1,0:T(8,128)(2,1)}, u32[]{:S(2)}) %copy-start) | copy-done | bytes 4194328
  137.2 0.0 copy-start.1
  137.2 2.2 %copy-done.1 = bf16[4,256,2048]{2,1,0:T(8,128)(2,1)S(1)} copy-done((bf16[4,256,2048]{2,1,0:T(8,128)(2,1)S(1)}, bf16[4,256,2048]{2,1,0:T(8,128)(2,1)}, u32[]{:S(2)}) %copy-start.1) | copy-done | bytes 4194328
  139.4 0.0 copy-start.2
  139.4 1.1 copy-done.2
  140.5 4.9 %weight_grads.1 = (bf16[2048,256]{1,0:T(8,128)(2,1)}, bf16[2048,256]{1,0:T(8,128)(2,1)}, bf16[32,2048]{1,0:T(8,128)(2,1)}, bf16[32,2048]{1,0:T(8,128)(2,1)}, bf16[256,512]{1,0:T(8,128)(2,1)}) custom-call(bf16[4,256,2048]{2,1,0:T(8,128)(2,1)S(1)} %copy-done, bf16[4,256,2048]{2,1,0:T(8,128)(2,1)S(1)} %copy-done.1, bf16[4,320,256]{2,1,0:T(8,128)(2,1)S(1)} %copy-done.2, ...), custom_call_target="tpu_custom_call" | custom-call | tf_op jit(solution)/shard_map/weight_grads/pallas_call | solution.py:638
Async XLA Ops:
  0.6 1.0 copy-start.3
  1.7 1.0 copy-start.4
  2.7 0.8 copy-start.5
  3.5 0.7 copy-start.6
  4.1 0.7 copy-start.7
  135.1 2.2 %copy-start = (bf16[4,256,2048]{2,1,0:T(8,128)(2,1)S(1)}, bf16[4,256,2048]{2,1,0:T(8,128)(2,1)}, u32[]{:S(2)}) copy-start(bf16[4,256,2048]{2,1,0:T(8,128)(2,1)} %get-tuple-element.15.tok) | copy-start | bytes 12582916
  137.2 2.2 %copy-start.1 = (bf16[4,256,2048]{2,1,0:T(8,128)(2,1)S(1)}, bf16[4,256,2048]{2,1,0:T(8,128)(2,1)}, u32[]{:S(2)}) copy-start(bf16[4,256,2048]{2,1,0:T(8,128)(2,1)} %get-tuple-element.16.up) | copy-start | bytes 12582916
  139.4 1.1 copy-start.2

commit v2 on v1

--- a/solution.py
+++ b/solution.py
@@ -53,10 +53,10 @@
     late, cot, early, lens, gain, w_q, w_k, w_v, w_o, freq,
     gin, tok_g, up_g, d_g, c_g,
     tok, wq, wkv, wo, up, part,
-    xq, xkv, dctx, probs, qs, kv_all, kvp_send, kvp_recv, cosv, sinv, inv_ref, cs_ref,
+    xq, xkv, dctx, probs, dss, qs, qs_t, kv_all, kvp_send, kvp_recv, cosv, sinv, inv_ref, cs_ref,
     aq, akv, dqkv, ctx,
-    rrel, racc, rdir, summed, rrel2, racc2, rdir2,
-    load_sem, up_sem, loc_sem, send_sem, recv_sem,
+    rrel, racc, rdir, summed, rrel2, racc2, rdir2, hop, stage, cot_stage, cot_part,
+    load_sem, up_sem, stage_sem, loc_sem, send_sem, recv_sem,
 ):
     s = lax.axis_index("section")
     d = lax.axis_index("dp")
@@ -87,15 +87,8 @@
             w_q.at[pl.ds(i * CHUNK, CHUNK), :], wq.at[pl.ds(i * CHUNK, CHUNK), :], load_sem.at[1, i]
         )
 
-    def wk_copy(i):
-        return pltpu.make_async_copy(
-            w_k.at[:, pl.ds(i * CHUNK, CHUNK)], wkv.at[0:32, pl.ds(i * CHUNK, CHUNK)], load_sem.at[2, i]
-        )
-
-    def wv_copy(i):
-        return pltpu.make_async_copy(
-            w_v.at[:, pl.ds(i * CHUNK, CHUNK)], wkv.at[32:64, pl.ds(i * CHUNK, CHUNK)], load_sem.at[3, i]
-        )
+    wk_copy = pltpu.make_async_copy(w_k, wkv.at[0:32, :], load_sem.at[2, 0])
+    wv_copy = pltpu.make_async_copy(w_v, wkv.at[32:64, :], load_sem.at[3, 0])
 
     def wo_copy(i):
         return pltpu.make_async_copy(
@@ -111,26 +104,50 @@
         pl.when(is_later)(later)
         pl.when(is_earlier)(earlier)
 
+    wk_copy.start()
+    wv_copy.start()
     for i in range(N_CHUNK):
         per_section(lambda: tok_copy(late, i).start(), lambda: tok_copy(early, i).start())
+    for i in range(N_CHUNK):
         wq_copy(i).start()
-        wk_copy(i).start()
-        wv_copy(i).start()
-    for i in range(N_CHUNK):
-        wo_copy(i).start()
-
-    @pl.when(is_later)
-    def _():
-        for yy in range(4):
-            for zz in range(4):
-                cot_copy(yy, zz).start()
+
+    def cols(index):
+        return pl.ds(pl.multiple_of(index * BLOCK, BLOCK), BLOCK)
+
+    def quarter(index, zz):
+        return pl.ds(pl.multiple_of(index * BLOCK + zz * TILE, TILE), TILE)
+
+    def stage_copy(source, o):
+        return pltpu.make_async_copy(source.at[:, cols(d_of[o])], stage.at[o - 2], stage_sem.at[0, o - 2])
+
+    def cot_stage_copy(o):
+        return pltpu.make_async_copy(
+            cot.at[:, quarter(d_of[o], z)], cot_stage.at[o - 2], stage_sem.at[1, o - 2]
+        )
+
+    def load_rest():
+        for i in range(N_CHUNK):
+            wo_copy(i).start()
+
+        @pl.when(is_later)
+        def _():
+            for yy in range(4):
+                for zz in range(4):
+                    cot_copy(yy, zz).start()
+
+        @pl.when(is_earlier)
+        def _():
+            for o in (2, 3):
+                cot_stage_copy(o).start()
+
+        for o in (2, 3):
+            per_section(lambda: stage_copy(early, o).start(), lambda: stage_copy(late, o).start())
 
     barrier = pltpu.get_barrier_semaphore()
     greeted = [z_peer[1], z_peer[2], z_peer[3], y_right, y_left, hand_peer]
     greeted += dp_peer[1:] + cross_peer[2:]
     for peer in greeted:
         pl.semaphore_signal(barrier, inc=1, device_id=peer, device_id_type=MESH)
-    pl.semaphore_wait(barrier, len(greeted))
 
     count = [0]
 
@@ -144,43 +161,133 @@
             device_id=peer, device_id_type=MESH,
         )
 
-    def cols(index):
-        return pl.ds(pl.multiple_of(index * BLOCK, BLOCK), BLOCK)
+    xkv[...] = jnp.zeros_like(xkv)
+    inv_ref[...] = jnp.zeros_like(inv_ref)
+
+    def scaled(span):
+        return (tok[:, span].astype(F32) * gain[0:1, span].astype(F32)).astype(BF16)
+
+    def project_kv(i, carry):
+        span = pl.ds(pl.multiple_of(i * CHUNK, CHUNK), CHUNK)
+        tok_copy(late, i).wait()
+        t = tok[:, span].astype(F32)
+        inv_ref[...] += jnp.sum(t * t, axis=1, keepdims=True)
+        xkv[...] += dot_nt(scaled(span), wkv[:, span])
+        return carry
+
+    wk_copy.wait()
+    wv_copy.wait()
+    lax.fori_loop(0, N_CHUNK, project_kv, 0, unroll=2)
+    inv_ref[...] = lax.rsqrt(inv_ref[...] * (1.0 / D) + 1e-5)
+    inv = inv_ref[:, 0:1]
+
+    kv_all[z] = jnp.transpose(xkv[...] * inv).astype(BF16)
+    pl.semaphore_wait(barrier, len(greeted))
+    kv_slots = [None] + [slot() for _ in range(3)]
+    kv_copies = [remote(kv_all.at[z], kv_all.at[z], kv_slots[o], z_peer[o]) for o in (1, 2, 3)]
+    for copy in kv_copies:
+        copy.start()
 
     tok_slots = [None] + [slot() for _ in range(3)]
     up_slots = [None] + [slot() for _ in range(3)]
-
-    def tok_send(source, o):
-        peer = dp_peer[1] if o == 1 else cross_peer[o]
-        return remote(source.at[:, cols(d_of[o])], tok_g.at[d], tok_slots[o], peer)
-
-    def cot_send(o):
-        peer = dp_peer[1] if o == 1 else cross_peer[o]
-        return remote(cot.at[:, cols(d_of[o])], up_g.at[d], up_slots[o], peer)
-
-    def tok_keep(source):
-        return pltpu.make_async_copy(source.at[:, cols(d)], tok_g.at[d], loc_sem.at[0])
-
-    def cot_keep():
-        return pltpu.make_async_copy(cot.at[:, cols(d)], up_g.at[d], loc_sem.at[1])
-
-    def later_starts():
-        tok_send(late, 1).start()
-        tok_send(early, 2).start()
-        tok_send(early, 3).start()
-        cot_send(1).start()
-        tok_keep(late).start()
-        cot_keep().start()
-
-    def earlier_starts():
-        tok_send(early, 1).start()
-        tok_send(late, 2).start()
-        tok_send(late, 3).start()
-        cot_send(2).start()
-        cot_send(3).start()
-        tok_keep(early).start()
-
-    per_section(later_starts, earlier_starts)
+    cot_slots = [None, None, slot(), slot()]
+    share_slots = [[slot() for _ in range(3)] for _ in range(2)]
+
+    def tok_send(o):
+        if o == 1:
+            return remote(tok.at[:, cols(d_of[1])], tok_g.at[d], tok_slots[1], dp_peer[1])
+        return remote(stage.at[o - 2], tok_g.at[d], tok_slots[o], cross_peer[o])
+
+    def tok_keep():
+        return pltpu.make_async_copy(tok.at[:, cols(d)], tok_g.at[d], loc_sem.at[0])
+
+    def up_send(o, zz):
+        return remote(up.at[d_of[o], zz], up_g.at[d, :, quarter(0, zz)], up_slots[o], dp_peer[o])
+
+    def up_keep(zz):
+        return pltpu.make_async_copy(up.at[d, zz], up_g.at[d, :, quarter(0, zz)], loc_sem.at[1])
+
+    def whole_block(o):
+        return remote(stage.at[0], up_g.at[d], up_slots[o], dp_peer[o])
+
+    def whole_keep():
+        return pltpu.make_async_copy(stage.at[0], up_g.at[d], loc_sem.at[1])
+
+    def cot_quarter(o):
+        return remote(cot_stage.at[o - 2], cot_part.at[o - 2], cot_slots[o], cross_peer[o])
+
+    def cot_share(o, p):
+        return remote(
+            cot_part.at[o - 2], up_g.at[d_of[o], :, quarter(0, z)], share_slots[o - 2][p - 1], z_peer[p]
+        )
+
+    def cot_keep(o):
+        return pltpu.make_async_copy(
+            cot_part.at[o - 2], up_g.at[d_of[o], :, quarter(0, z)], loc_sem.at[o + 2]
+        )
+
+    def send_operands():
+        @pl.when(is_earlier)
+        def _():
+            for o in (2, 3):
+                cot_stage_copy(o).wait()
+                cot_quarter(o).start()
+
+        for o in (2, 3):
+            stage_copy(early, o).wait()
+            tok_send(o).start()
+        tok_send(1).start()
+        tok_keep().start()
+
+    load_rest()
+    sent = list(kv_copies)
+    received = []
+
+    def finish():
+        for copy in sent:
+            copy.wait_send()
+        for copy in received:
+            copy.wait()
+
+        @pl.when(is_later)
+        def _():
+            for o in (2, 3):
+                for p in (1, 2, 3):
+                    cot_share(o, p).wait()
+                cot_keep(o).wait()
+                whole_block(o).wait_send()
+
+        @pl.when(is_earlier)
+        def _():
+            for o in (2, 3):
+                cot_quarter(o).wait_send()
+                for i in range(8):
+                    hop_send(o, i).wait_send()
+                whole_block(o).wait_recv()
+
+        whole_block(1).wait()
+        whole_keep().wait()
+        for o in (1, 2, 3):
+            tok_send(o).wait()
+        tok_keep().wait()
+
+    hop_slots = [None, None] + [[slot() for _ in range(8)] for _ in range(2)]
+
+    def hop_send(o, i):
+        zz, low = i // 2, i % 2 == 0
+        rows = pl.ds(0 if low else 128, 128)
+        return remote(
+            up.at[d_of[o], zz, rows, :], hop.at[o - 2, i], hop_slots[o][i], hand_peer if low else cross_peer[o]
+        )
+
+    def hop_on(o, i):
+        zz, low = i // 2, i % 2 == 0
+        rows = pl.ds(0 if low else 128, 128)
+        home = d if low else d_of[o]
+        return remote(
+            hop.at[o - 2, i], up_g.at[home, rows, pl.ds(zz * TILE, TILE)], up_slots[o],
+            cross_peer[o] if low else hand_peer,
+        )
 
     lane = lax.broadcasted_iota(jnp.int32, (SEQ, HD), 1)
     place = lax.broadcasted_iota(jnp.int32, (SEQ, HD), 0)
@@ -190,39 +297,24 @@
     sinv[...] = jnp.where(lane < 64, -1.0, 1.0) * jnp.sin(angle)
 
     xq[...] = jnp.zeros_like(xq)
-    xkv[...] = jnp.zeros_like(xkv)
-    inv_ref[...] = jnp.zeros_like(inv_ref)
-
-    def project(i, carry):
+
+    def project_q(i, carry):
         span = pl.ds(pl.multiple_of(i * CHUNK, CHUNK), CHUNK)
-        tok_copy(late, i).wait()
         wq_copy(i).wait()
-        wk_copy(i).wait()
-        wv_copy(i).wait()
-        t = tok[:, span].astype(F32)
-        x = (t * gain[0:1, span].astype(F32)).astype(BF16)
-        inv_ref[...] += jnp.sum(t * t, axis=1, keepdims=True)
-        xq[...] += dot_nn(x, wq[span, :])
-        xkv[...] += dot_nt(x, wkv[:, span])
+        xq[...] += dot_nn(scaled(span), wq[span, :])
         return carry
 
-    lax.fori_loop(0, N_CHUNK, project, 0)
-    inv_ref[...] = lax.rsqrt(inv_ref[...] * (1.0 / D) + 1e-5)
-    inv = inv_ref[:, 0:1]
-
-    kv_all[z] = jnp.transpose(xkv[...] * inv).astype(BF16)
-    kv_slots = [None] + [slot() for _ in range(3)]
-    kv_copies = [remote(kv_all.at[z], kv_all.at[z], kv_slots[o], z_peer[o]) for o in (1, 2, 3)]
-    for copy in kv_copies:
-        copy.start()
-
+    lax.fori_loop(0, N_CHUNK, project_q, 0, unroll=2)
     cos = cosv[...]
     sin = sinv[...]
     cos_t = jnp.transpose(cos)
     sin_t = jnp.transpose(sin)
     for j in range(2):
         q = xq[:, j * HD:(j + 1) * HD] * inv
-        qs[j] = (q * cos + pltpu.roll(q, 64, 1) * sin).astype(BF16)
+        q = q * cos + pltpu.roll(q, 64, 1) * sin
+        qs[j] = q.astype(BF16)
+        qs_t[j] = jnp.transpose(q).astype(BF16)
+    inv_t = jnp.transpose(inv_ref[...])[0:1, :]
     for copy in kv_copies:
         copy.wait_recv()
     k = jnp.concatenate([kv_all[i, 0:32] for i in range(4)], axis=0).astype(F32)
@@ -245,6 +337,8 @@
     for copy in ctx_copies:
         copy.start()
     ctx_keep.start()
+    received += ctx_copies + [ctx_keep]
+    send_operands()
 
     for i in range(N_CHUNK):
         wo_copy(i).wait()
@@ -259,25 +353,31 @@
     def add_context(k, yy, zz):
         dctx[halves(k), :] += dot_nn(up[yy, zz, halves(k), :], wo[wo_rows(yy, zz), :])
 
-    own_slots = [slot() for _ in range(2)]
+    own_slots = [slot() for _ in range(4)]
     p1_slots = [[slot() for _ in range(4)] for _ in range(2)]
     p2_slots = [[[slot() for _ in range(4)] for _ in range(4)] for _ in range(2)]
 
-    def hand_copy(k):
-        return remote(up.at[y, z, halves(k), :], up.at[y, z, halves(k), :], own_slots[k], hand_peer)
+    def rows_of(g):
+        return pl.ds(g * 64, 64)
+
+    def hand_copy(g):
+        return remote(gin.at[rows_of(g), :], up.at[y, z, rows_of(g), :], own_slots[g], hand_peer)
 
     def at(k, first, second):
         return (second, first) if k == 0 else (first, second)
 
     @pl.when(is_later)
     def _():
-        def body(i, carry):
-            yy, zz = lax.div(i, 4), lax.rem(i, 4)
-            cot_copy(yy, zz).wait()
-            dctx[...] += dot_nn(up[yy, zz], wo[wo_rows(yy, zz), :])
+        def body(yy, carry):
+            total = dctx[...]
+            for zz in range(4):
+                cot_copy(yy, zz).wait()
+            for zz in range(4):
+                total += dot_nn(up[yy, zz], wo[wo_rows(yy, zz), :])
+            dctx[...] = total
             return carry
 
-        lax.fori_loop(0, 16, body, 0)
+        lax.fori_loop(0, 4, body, 0)
 
     @pl.when(is_earlier)
     def _():
@@ -306,7 +406,8 @@
             send(k, a, second_of[k], 0, 128, p2_slots[k][o][1], second_left[k])
 
         for k in range(2):
-            hand_copy(k).wait_recv()
+            hand_copy(2 * k).wait_recv()
+            hand_copy(2 * k + 1).wait_recv()
             send(k, first_of[k], second_of[k], 0, 128, p1_slots[k][0], first_right[k])
             send(k, first_of[k], second_of[k], 0, 128, p1_slots[k][1], first_left[k])
             spread(k, 0)
@@ -354,26 +455,22 @@
                 add_context(k, *at(k, a, b))
         for copy in pending:
             copy.wait_send()
-        for o in (2, 3, 1):
-            for zz in range(4):
-                remote(
-                    up.at[d_of[o], zz], up_g.at[d, :, pl.ds(zz * TILE, TILE)], up_slots[o], dp_peer[o]
-                ).start()
-        for zz in range(4):
-            pltpu.make_async_copy(up.at[d, zz], up_g.at[d, :, pl.ds(zz * TILE, TILE)], loc_sem.at[1]).start()
+        for i in range(8):
+            for o in (2, 3):
+                hop_send(o, i).start()
+
+    for zz in range(4):
+        up_send(1, zz).start()
+        up_keep(zz).start()
 
     dk_t = jnp.zeros((HD, SEQ), F32)
     dv_t = jnp.zeros((HD, SEQ), F32)
-    dq_list = []
     for j in range(2):
         grad = dctx[:, j * HD:(j + 1) * HD]
-        grad_low = grad.astype(BF16)
         pr = probs[j]
-        dp = dot_nn(grad_low, v_t)
-        ds = (pr * (dp - jnp.sum(dp * pr, axis=1, keepdims=True)) * SCALE).astype(BF16)
-        dq = dot_nt(k_t, ds)
-        dq_list.append(dq * cos_t - swap_rows(dq) * sin_t)
-        dk_t += dot_nn(jnp.transpose(qs[j].astype(F32)).astype(BF16), ds)
+        dp = dot_nn(grad.astype(BF16), v_t)
+        dss[j] = (pr * (dp - jnp.sum(dp * pr, axis=1, keepdims=True)) * SCALE).astype(BF16)
+        dk_t += dot_nn(qs_t[j], dss[j])
         dv_t += dot_nn(jnp.transpose(grad).astype(BF16), pr.astype(BF16))
     dk_t = dk_t * cos_t - swap_rows(dk_t) * sin_t
     for i in range(4):
@@ -385,7 +482,11 @@
     ]
     for copy in kvp_copies:
         copy.start()
-    inv_t = jnp.transpose(inv_ref[...])[0:1, :]
+    sent += kvp_copies
+    dq_list = []
+    for j in range(2):
+        dq = dot_nt(k_t, dss[j])
+        dq_list.append(dq * cos_t - swap_rows(dq) * sin_t)
     dq_t = jnp.concatenate(dq_list, axis=0)
     dqkv[0:256, :] = (dq_t * inv_t).astype(BF16)
     dq = jnp.transpose(dq_t)
@@ -407,154 +508,160 @@
     for copy in d_copies:
         copy.start()
     d_keep.start()
+    received += d_copies + [d_keep]
 
     ring_of, other_of = (y, z), (z, y)
     right_1, left_1 = (y_right, z_right), (y_left, z_left)
     right_2, left_2 = (z_right, y_right), (z_left, y_left)
 
-    def block(k, a, lo, n):
-        if k == 0:
-            return part.at[a, pl.ds(lo, n), halves(k), :]
-        return part.at[pl.ds(lo, n), a, halves(k), :]
+    def block(g, a, lo, n):
+        if g < 2:
+            return part.at[a, pl.ds(lo, n), rows_of(g), :]
+        return part.at[pl.ds(lo, n), a, rows_of(g), :]
 
     def tile(k, a, b):
         return (a, b) if k == 0 else (b, a)
 
-    def compute(k, a):
-        def body(b, carry):
-            yy, zz = tile(k, a, b)
+    def compute(*tiles):
+        for dy, dz in tiles:
+            yy, zz = ring(y + dy), ring(z + dz)
             span = wo_rows(yy, zz)
-            total = dot_nt(aq[halves(k), :], wq[span, :]) + dot_nn(akv[halves(k), :], wkv[:, span])
-            total = total * gain[0:1, span].astype(F32) - tok[halves(k), span].astype(F32) * cs_ref[halves(k), 0:1]
-            part[yy, zz, halves(k), :] = total.astype(BF16)
-            return carry
-
-        lax.fori_loop(0, 4, body, 0)
-
-    rs1 = [[slot() for _ in range(6)] for _ in range(2)]
-    rs2 = [[slot() for _ in range(6)] for _ in range(2)]
-    sent = []
+            total = dot_nt(aq[...], wq[span, :]) + dot_nn(akv[...], wkv[:, span])
+            total = total * gain[0:1, span].astype(F32) - tok[:, span].astype(F32) * cs_ref[:, 0:1]
+            part[yy, zz] = total.astype(BF16)
+
+    rs1 = [[slot() for _ in range(6)] for _ in range(4)]
+    rs2 = [[slot() for _ in range(6)] for _ in range(4)]
 
     def go(src, dst, n, peer):
         copy = remote(src, dst, n, peer)
         copy.start()
         sent.append(copy)
 
-    for k in range(2):
-        i = ring_of[k]
-        compute(k, ring(i + 2))
-        go(block(k, ring(i + 2), 0, 2), rrel.at[k, 0:2], rs1[k][0], right_1[k])
-        go(block(k, ring(i + 2), 2, 2), rrel.at[k, 2:4], rs1[k][1], left_1[k])
-    for k in range(2):
-        i = ring_of[k]
-        compute(k, ring(i + 1))
-        go(block(k, ring(i + 1), 2, 2), rdir.at[k, 2:4], rs1[k][5], right_1[k])
-        compute(k, ring(i - 1))
-        go(block(k, ring(i - 1), 0, 2), rdir.at[k, 0:2], rs1[k][4], left_1[k])
-    for k in range(2):
-        compute(k, ring_of[k])
-
     def landed(ref, n):
         remote(ref, ref, n, y_right).wait_recv()
 
-    for k in range(2):
-        i = ring_of[k]
-        landed(rrel.at[k, 0:2], rs1[k][0])
+    def relay_1(g):
+        k, i = g // 2, ring_of[g // 2]
+        go(block(g, ring(i + 2), 0, 2), rrel.at[g, 0:2], rs1[g][0], right_1[k])
+        go(block(g, ring(i + 2), 2, 2), rrel.at[g, 2:4], rs1[g][1], left_1[k])
+
+    def direct_right_1(g):
+        k, i = g // 2, ring_of[g // 2]
+        go(block(g, ring(i + 1), 2, 2), rdir.at[g, 2:4], rs1[g][5], right_1[k])
+
+    def direct_left_1(g):
+        k, i = g // 2, ring_of[g // 2]
+        go(block(g, ring(i - 1), 0, 2), rdir.at[g, 0:2], rs1[g][4], left_1[k])
+
+    def add_relay(g, a, b):
+        yy, zz = tile(g // 2, a, b)
+        part[yy, zz, rows_of(g), :] = (
+            part[yy, zz, rows_of(g), :].astype(F32) + rrel[g, b].astype(F32)
+        ).astype(BF16)
+
+    def accumulate_1(g):
+        k, i = g // 2, ring_of[g // 2]
+        landed(rrel.at[g, 0:2], rs1[g][0])
         for b in range(2):
-            yy, zz = tile(k, ring(i + 1), b)
-            part[yy, zz, halves(k), :] = (
-                part[yy, zz, halves(k), :].astype(F32) + rrel[k, b].astype(F32)
-            ).astype(BF16)
-        go(block(k, ring(i + 1), 0, 2), racc.at[k, 0:2], rs1[k][2], right_1[k])
-        landed(rrel.at[k, 2:4], rs1[k][1])
+            add_relay(g, ring(i + 1), b)
+        go(block(g, ring(i + 1), 0, 2), racc.at[g, 0:2], rs1[g][2], right_1[k])
+        landed(rrel.at[g, 2:4], rs1[g][1])
         for b in range(2, 4):
-            yy, zz = tile(k, ring(i - 1), b)
-            part[yy, zz, halves(k), :] = (
-                part[yy, zz, halves(k), :].astype(F32) + rrel[k, b].astype(F32)
-            ).astype(BF16)
-        go(block(k, ring(i - 1), 2, 2), racc.at[k, 2:4], rs1[k][3], left_1[k])
-
-    def collect(k, b):
-        yy, zz = tile(k, ring_of[k], b)
-        summed[k, b] = (
-            part[yy, zz, halves(k), :].astype(F32) + racc[k, b].astype(F32) + rdir[k, b].astype(F32)
+            add_relay(g, ring(i - 1), b)
+        go(block(g, ring(i - 1), 2, 2), racc.at[g, 2:4], rs1[g][3], left_1[k])
+
+    def collect(g, b):
+        yy, zz = tile(g // 2, ring_of[g // 2], b)
+        summed[g, b] = (
+            part[yy, zz, rows_of(g), :].astype(F32) + racc[g, b].astype(F32) + rdir[g, b].astype(F32)
         ).astype(BF16)
 
-    for k in range(2):
-        j = other_of[k]
-        landed(rdir.at[k, 0:2], rs1[k][4])
-        landed(rdir.at[k, 2:4], rs1[k][5])
-        landed(racc.at[k, 0:2], rs1[k][2])
-        landed(racc.at[k, 2:4], rs1[k][3])
-        collect(k, ring(j + 2))
-        go(summed.at[k, ring(j + 2), 0:64], rrel2.at[k, 0:64], rs2[k][0], right_2[k])
-        go(summed.at[k, ring(j + 2), 64:128], rrel2.at[k, 64:128], rs2[k][1], left_2[k])
-        collect(k, ring(j + 1))
-        go(summed.at[k, ring(j + 1), 64:128], rdir2.at[k, 64:128], rs2[k][5], right_2[k])
-        collect(k, ring(j - 1))
-        go(summed.at[k, ring(j - 1), 0:64], rdir2.at[k, 0:64], rs2[k][4], left_2[k])
-        collect(k, j)
-    for k in range(2):
-        j = other_of[k]
-        landed(rrel2.at[k, 0:64], rs2[k][0])
+    def turn(g):
+        k, j = g // 2, other_of[g // 2]
+        landed(rdir.at[g, 0:2], rs1[g][4])
+        landed(rdir.at[g, 2:4], rs1[g][5])
+        landed(racc.at[g, 0:2], rs1[g][2])
+        landed(racc.at[g, 2:4], rs1[g][3])
+        collect(g, ring(j + 2))
+        go(summed.at[g, ring(j + 2), 0:32], rrel2.at[g, 0:32], rs2[g][0], right_2[k])
+        go(summed.at[g, ring(j + 2), 32:64], rrel2.at[g, 32:64], rs2[g][1], left_2[k])
+        collect(g, ring(j + 1))
+        go(summed.at[g, ring(j + 1), 32:64], rdir2.at[g, 32:64], rs2[g][5], right_2[k])
+        collect(g, ring(j - 1))
+        go(summed.at[g, ring(j - 1), 0:32], rdir2.at[g, 0:32], rs2[g][4], left_2[k])
+        collect(g, j)
+
+    def accumulate_2(g):
+        k, j = g // 2, other_of[g // 2]
+        landed(rrel2.at[g, 0:32], rs2[g][0])
         a = ring(j + 1)
-        summed[k, a, 0:64] = (summed[k, a, 0:64].astype(F32) + rrel2[k, 0:64].astype(F32)).astype(BF16)
-        go(summed.at[k, a, 0:64], racc2.at[k, 0:64], rs2[k][2], right_2[k])
-        landed(rrel2.at[k, 64:128], rs2[k][1])
+        summed[g, a, 0:32] = (summed[g, a, 0:32].astype(F32) + rrel2[g, 0:32].astype(F32)).astype(BF16)
+        go(summed.at[g, a, 0:32], racc2.at[g, 0:32], rs2[g][2], right_2[k])
+        landed(rrel2.at[g, 32:64], rs2[g][1])
         a = ring(j - 1)
-        summed[k, a, 64:128] = (summed[k, a, 64:128].astype(F32) + rrel2[k, 64:128].astype(F32)).astype(BF16)
-        go(summed.at[k, a, 64:128], racc2.at[k, 64:128], rs2[k][3], left_2[k])
-    for k in range(2):
-        j = other_of[k]
-        landed(rdir2.at[k, 0:64], rs2[k][4])
-        landed(rdir2.at[k, 64:128], rs2[k][5])
-        landed(racc2.at[k, 0:64], rs2[k][2])
-        landed(racc2.at[k, 64:128], rs2[k][3])
-        gin[halves(k), :] = (
-            up[y, z, halves(k), :].astype(F32)
-            + summed[k, j].astype(F32)
-            + racc2[k].astype(F32)
-            + rdir2[k].astype(F32)
+        summed[g, a, 32:64] = (summed[g, a, 32:64].astype(F32) + rrel2[g, 32:64].astype(F32)).astype(BF16)
+        go(summed.at[g, a, 32:64], racc2.at[g, 32:64], rs2[g][3], left_2[k])
+
+    def result(g):
+        j = other_of[g // 2]
+        landed(rdir2.at[g, 0:32], rs2[g][4])
+        landed(rdir2.at[g, 32:64], rs2[g][5])
+        landed(racc2.at[g, 0:32], rs2[g][2])
+        landed(racc2.at[g, 32:64], rs2[g][3])
+        gin[rows_of(g), :] = (
+            up[y, z, rows_of(g), :].astype(F32)
+            + summed[g, j].astype(F32)
+            + racc2[g].astype(F32)
+            + rdir2[g].astype(F32)
         ).astype(BF16)
-
-        @pl.when(is_later)
-        def _():
-            remote(gin.at[halves(k), :], up.at[y, z, halves(k), :], own_slots[k], hand_peer).start()
-
-    for copy in sent + kv_copies + ctx_copies + kvp_copies + d_copies:
-        copy.wait_send()
-    for copy in ctx_copies + d_copies:
-        copy.wait_recv()
-    ctx_keep.wait()
-    d_keep.wait()
+        pl.when(is_later)(lambda: hand_copy(g).start())
+
+    def each(step, *groups):
+        for g in groups:
+            step(g)
+
+    compute((2, 2), (2, 1), (2, 3), (2, 0))
+    each(relay_1, 0, 1)
+    compute((1, 2), (3, 2), (0, 2))
+    each(relay_1, 2, 3)
+    compute((1, 1), (1, 3), (1, 0))
+    direct_right_1(0)
+    compute((3, 1), (3, 3), (3, 0))
+    direct_left_1(0)
+    compute((0, 1), (0, 3))
+    each(direct_right_1, 2)
+    each(direct_left_1, 2)
+    each(accumulate_1, 0, 2)
+    each(direct_right_1, 1, 3)
+    each(direct_left_1, 1, 3)
+    compute((0, 0))
+    each(accumulate_1, 1, 3)
+    each(turn, 0, 2)
+    each(accumulate_2, 0, 2)
+    each(turn, 1, 3)
+    each(result, 0, 2)
+    each(accumulate_2, 1, 3)
+    each(result, 1, 3)
 
     @pl.when(is_later)
     def _():
-        for k in range(2):
-            hand_copy(k).wait_send()
-
-    tok_keep(late).wait()
-    cot_keep().wait()
-    for o in (1, 2, 3):
-        copy = tok_send(late, o)
-        copy.wait_send()
-        copy.wait_recv()
-        copy = cot_send(o)
-        copy.wait_recv()
-
-    @pl.when(is_later)
-    def _():
-        cot_send(1).wait_send()
-
-    @pl.when(is_earlier)
-    def _():
-        for o in (1, 2, 3):
-            cot_send(o).wait_send()
         for o in (2, 3):
-            cot_send(o).wait_send()
-
-
-N_SLOTS = 6 + 3 + 3 + 2 + 8 + 32 + 3 + 3 + 24
+            cot_quarter(o).wait_recv()
+            for p in (1, 2, 3):
+                cot_share(o, p).start()
+            cot_keep(o).start()
+        for i in range(8):
+            for o in (2, 3):
+                hop_send(o, i).wait_recv()
+                hop_on(o, i).start()
+        for g in range(4):
+            hand_copy(g).wait_send()
+
+    finish()
+
+
+N_SLOTS = 6 + 3 + 2 + 6 + 16 + 3 + 4 + 8 + 32 + 3 + 3 + 48
 
 
 def relay(late, cot, early, lens, gain, w_q, w_k, w_v, w_o, freq):
@@ -579,7 +686,9 @@
         pltpu.VMEM((SEQ, KV), F32),
         pltpu.VMEM((SEQ, 256), F32),
         pltpu.VMEM((2, SEQ, SEQ), F32),
+        pltpu.VMEM((2, SEQ, SEQ), BF16),
         pltpu.VMEM((2, SEQ, HD), BF16),
+        pltpu.VMEM((2, HD, SEQ), BF16),
         pltpu.VMEM((4, KV, SEQ), BF16),
         pltpu.VMEM((4, KV, SEQ), BF16),
         pltpu.VMEM((4, KV, SEQ), BF16),
@@ -591,16 +700,21 @@
         pltpu.VMEM((SEQ, KV), BF16),
         pltpu.VMEM((ROWS, SEQ), BF16),
         pltpu.VMEM((256, SEQ), BF16),
-        pltpu.VMEM((2, 4, 128, TILE), BF16),
-        pltpu.VMEM((2, 4, 128, TILE), BF16),
-        pltpu.VMEM((2, 4, 128, TILE), BF16),
-        pltpu.VMEM((2, 4, 128, TILE), BF16),
-        pltpu.VMEM((2, 128, TILE), BF16),
-        pltpu.VMEM((2, 128, TILE), BF16),
-        pltpu.VMEM((2, 128, TILE), BF16),
+        pltpu.VMEM((4, 4, 64, TILE), BF16),
+        pltpu.VMEM((4, 4, 64, TILE), BF16),
+        pltpu.VMEM((4, 4, 64, TILE), BF16),
+        pltpu.VMEM((4, 4, 64, TILE), BF16),
+        pltpu.VMEM((4, 64, TILE), BF16),
+        pltpu.VMEM((4, 64, TILE), BF16),
+        pltpu.VMEM((4, 64, TILE), BF16),
+        pltpu.VMEM((2, 8, 128, TILE), BF16),
+        pltpu.VMEM((2, SEQ, BLOCK), BF16),
+        pltpu.VMEM((2, SEQ, TILE), BF16),
+        pltpu.VMEM((2, SEQ, TILE), BF16),
         pltpu.SemaphoreType.DMA((5, N_CHUNK)),
         pltpu.SemaphoreType.DMA((4, 4)),
-        pltpu.SemaphoreType.DMA((4,)),
+        pltpu.SemaphoreType.DMA((2, 2)),
+        pltpu.SemaphoreType.DMA((6,)),
         pltpu.SemaphoreType.DMA((N_SLOTS,)),
         pltpu.SemaphoreType.DMA((N_SLOTS,)),
     ]
@@ -611,7 +725,7 @@
         out_specs=(vmem, any_spec, any_spec, any_spec, any_spec),
         scratch_shapes=scratch,
         compiler_params=pltpu.CompilerParams(
-            collective_id=0, has_side_effects=True, vmem_limit_bytes=52 * 1024 * 1024
+            collective_id=0, has_side_effects=True, vmem_limit_bytes=62 * 1024 * 1024
         ),
         name="relay",
     )(late, cot, early, lens, gain, w_q, w_k, w_v, w_o, freq)
@@ -660,7 +774,7 @@
             pl.BlockSpec((32, TILE), lambda i: (0, i)),
             pl.BlockSpec((SEQ, TILE), lambda i: (0, 0)),
         ),
-        compiler_params=pltpu.CompilerParams(vmem_limit_bytes=40 * 1024 * 1024),
+        compiler_params=pltpu.CompilerParams(vmem_limit_bytes=62 * 1024 * 1024),
         name="weight_grads",
     )(tok_g, up_g, d_g, c_g, gain, gin)
 

time: 148 us -> 126 us (0.85)
  Pallas kernels: 135 us -> 123 us
  local copies, waits for them, and re-layouts: 9.6 us -> 0 us
    pallas_call x1, Pallas kernels: 130 us -> 116 us  [relay(): pl.pallas_call(relay_kernel, out_shape=out_shape, in_specs=[any_spec, any...]
    unnamed x16 -> x0, local copies, waits for them, and re-layouts: 9.6 us -> none
    pallas_call x1, Pallas kernels: 4.86 us -> 7.13 us  [weight_grads(): pl.pallas_call(weights_kernel, grid=(4,), out_shape=(jax.ShapeDtypeStruct...]
where the time goes in v2:
time: 126 us; the launch traced here: 124 us
  Pallas kernels  123 us (98%)
    pallas_call x1, Pallas kernels, relay(): pl.pallas_call(relay_kernel, out_shape=out_shape, in_specs=[any_spec, any...  116 us
    pallas_call x1, Pallas kernels, weight_grads(): pl.pallas_call(weights_kernel, grid=(4,), out_shape=(jax.ShapeDtypeStruct...  7.13 us

profile of v2, /device:TPU:0, one launch (start us, length us, event | category | flops | bytes accessed | tf_op | source)
XLA Modules:
  0.0 124.1 jit_solution(12075519771802170120)
XLA Ops:
  0.6 116.3 %relay.1 = (bf16[256,512]{1,0:T(8,128)(2,1)}, bf16[4,256,2048]{2,1,0:T(8,128)(2,1)}, bf16[4,256,2048]{2,1,0:T(8,128)(2,1)}, bf16[4,320,256]{2,1,0:T(8,128)(2,1)}, bf16[4,256,256]{2,1,0:T(8,128)(2,1)}) custom-call(bf16[256,8192]{1,0:T(8,128)(2,1)} %late.1, bf16[256,8192]{1,0:T(8,128)(2,1)} %cot.1, bf16[256,8192]{1,0:T(8,128)(2,1)} %early.1, s32[1,4]{1,0:T(1,128)} %lens.1, ...), custom_call_target="tpu_custom_call" | custom-call | tf_op jit(solution)/shard_map/relay/pallas_call | solution.py:721
  116.9 7.1 %weight_grads.1 = (bf16[2048,256]{1,0:T(8,128)(2,1)}, bf16[2048,256]{1,0:T(8,128)(2,1)}, bf16[32,2048]{1,0:T(8,128)(2,1)}, bf16[32,2048]{1,0:T(8,128)(2,1)}, bf16[256,512]{1,0:T(8,128)(2,1)}) custom-call(bf16[4,256,2048]{2,1,0:T(8,128)(2,1)} %get-tuple-element.15.tok, bf16[4,256,2048]{2,1,0:T(8,128)(2,1)} %get-tuple-element.16.up, ...), custom_call_target="tpu_custom_call" | custom-call | tf_op jit(solution)/shard_map/weight_grads/pallas_call | solution.py:752

commit v3 on v2

--- a/solution.py
+++ b/solution.py
@@ -55,7 +55,7 @@
     tok, wq, wkv, wo, up, part,
     xq, xkv, dctx, probs, dss, qs, qs_t, kv_all, kvp_send, kvp_recv, cosv, sinv, inv_ref, cs_ref,
     aq, akv, dqkv, ctx,
-    rrel, racc, rdir, summed, rrel2, racc2, rdir2, hop, stage, cot_stage, cot_part,
+    rrel, racc, rdir, summed, rrel2, racc2, rdir2, hop, tok_stage, tok_part, cot_stage, cot_part,
     load_sem, up_sem, stage_sem, loc_sem, send_sem, recv_sem,
 ):
     s = lax.axis_index("section")
@@ -71,7 +71,8 @@
         return {"mp": yy * 4 + zz}
 
     z_peer = [mp_id(y, ring(z + o)) for o in range(4)]
-    y_right, y_left = mp_id(ring(y + 1), z), mp_id(ring(y - 1), z)
+    y_peer = [mp_id(ring(y + o), z) for o in range(4)]
+    y_right, y_left = y_peer[1], y_peer[3]
     z_right, z_left = z_peer[1], z_peer[3]
     dp_peer = [{"dp": d_of[o]} for o in range(4)]
     cross_peer = [None, None] + [{"section": 1 - s, "dp": d_of[o]} for o in (2, 3)]
@@ -118,11 +119,13 @@
         return pl.ds(pl.multiple_of(index * BLOCK + zz * TILE, TILE), TILE)
 
     def stage_copy(source, o):
-        return pltpu.make_async_copy(source.at[:, cols(d_of[o])], stage.at[o - 2], stage_sem.at[0, o - 2])
+        return pltpu.make_async_copy(
+            source.at[:, quarter(d_of[o], z)], tok_stage.at[o - 2], stage_sem.at[0, o - 2]
+        )
 
     def cot_stage_copy(o):
         return pltpu.make_async_copy(
-            cot.at[:, quarter(d_of[o], z)], cot_stage.at[o - 2], stage_sem.at[1, o - 2]
+            cot.at[:, quarter(d_of[o], y)], cot_stage.at[o - 2], stage_sem.at[1, o - 2]
         )
 
     def load_rest():
@@ -144,7 +147,7 @@
             per_section(lambda: stage_copy(early, o).start(), lambda: stage_copy(late, o).start())
 
     barrier = pltpu.get_barrier_semaphore()
-    greeted = [z_peer[1], z_peer[2], z_peer[3], y_right, y_left, hand_peer]
+    greeted = z_peer[1:] + y_peer[1:] + [hand_peer]
     greeted += dp_peer[1:] + cross_peer[2:]
     for peer in greeted:
         pl.semaphore_signal(barrier, inc=1, device_id=peer, device_id_type=MESH)
@@ -192,11 +195,30 @@
     up_slots = [None] + [slot() for _ in range(3)]
     cot_slots = [None, None, slot(), slot()]
     share_slots = [[slot() for _ in range(3)] for _ in range(2)]
-
-    def tok_send(o):
-        if o == 1:
-            return remote(tok.at[:, cols(d_of[1])], tok_g.at[d], tok_slots[1], dp_peer[1])
-        return remote(stage.at[o - 2], tok_g.at[d], tok_slots[o], cross_peer[o])
+    tok_share_slots = [[slot() for _ in range(3)] for _ in range(2)]
+
+    def tok_send():
+        return remote(tok.at[:, cols(d_of[1])], tok_g.at[d], tok_slots[1], dp_peer[1])
+
+    def tok_quarter(o):
+        return remote(tok_stage.at[o - 2], tok_part.at[o - 2], tok_slots[o], cross_peer[o])
+
+    def tok_share(o, p):
+        return remote(
+            tok_part.at[o - 2], tok_g.at[d_of[o], :, quarter(0, z)], tok_share_slots[o - 2][p - 1], z_peer[p]
+        )
+
+    def tok_own(o):
+        return pltpu.make_async_copy(
+            tok_part.at[o - 2], tok_g.at[d_of[o], :, quarter(0, z)], loc_sem.at[o + 4]
+        )
+
+    def share_tok():
+        for o in (2, 3):
+            tok_quarter(o).wait_recv()
+            for p in (1, 2, 3):
+                tok_share(o, p).start()
+            tok_own(o).start()
 
     def tok_keep():
         return pltpu.make_async_copy(tok.at[:, cols(d)], tok_g.at[d], loc_sem.at[0])
@@ -208,22 +230,22 @@
         return pltpu.make_async_copy(up.at[d, zz], up_g.at[d, :, quarter(0, zz)], loc_sem.at[1])
 
     def whole_block(o):
-        return remote(stage.at[0], up_g.at[d], up_slots[o], dp_peer[o])
+        return remote(tok.at[:, pl.ds(0, BLOCK)], up_g.at[d], up_slots[o], dp_peer[o])
 
     def whole_keep():
-        return pltpu.make_async_copy(stage.at[0], up_g.at[d], loc_sem.at[1])
+        return pltpu.make_async_copy(tok.at[:, pl.ds(0, BLOCK)], up_g.at[d], loc_sem.at[1])
 
     def cot_quarter(o):
         return remote(cot_stage.at[o - 2], cot_part.at[o - 2], cot_slots[o], cross_peer[o])
 
     def cot_share(o, p):
         return remote(
-            cot_part.at[o - 2], up_g.at[d_of[o], :, quarter(0, z)], share_slots[o - 2][p - 1], z_peer[p]
+            cot_part.at[o - 2], up_g.at[d_of[o], :, quarter(0, y)], share_slots[o - 2][p - 1], y_peer[p]
         )
 
     def cot_keep(o):
         return pltpu.make_async_copy(
-            cot_part.at[o - 2], up_g.at[d_of[o], :, quarter(0, z)], loc_sem.at[o + 2]
+            cot_part.at[o - 2], up_g.at[d_of[o], :, quarter(0, y)], loc_sem.at[o + 2]
         )
 
     def send_operands():
@@ -235,8 +257,8 @@
 
         for o in (2, 3):
             stage_copy(early, o).wait()
-            tok_send(o).start()
-        tok_send(1).start()
+            tok_quarter(o).start()
+        tok_send().start()
         tok_keep().start()
 
     load_rest()
@@ -261,32 +283,36 @@
         def _():
             for o in (2, 3):
                 cot_quarter(o).wait_send()
-                for i in range(8):
-                    hop_send(o, i).wait_send()
                 whole_block(o).wait_recv()
+                for k in range(2):
+                    for zz in range(4):
+                        hop_in(o, k, 0, zz).wait_send()
+            for n, index in gathered:
+                ref = up.at[0, 0, pl.ds(0, n), :]
+                remote(ref, ref, index, hand_peer).wait_send()
 
         whole_block(1).wait()
         whole_keep().wait()
-        for o in (1, 2, 3):
-            tok_send(o).wait()
+        tok_send().wait()
         tok_keep().wait()
-
-    hop_slots = [None, None] + [[slot() for _ in range(8)] for _ in range(2)]
-
-    def hop_send(o, i):
-        zz, low = i // 2, i % 2 == 0
-        rows = pl.ds(0 if low else 128, 128)
+        for o in (2, 3):
+            tok_quarter(o).wait_send()
+            for p in (1, 2, 3):
+                tok_share(o, p).wait()
+            tok_own(o).wait()
+
+    hop_slots = [None, None] + [[[slot() for _ in range(4)][0] for _ in range(2)] for _ in range(2)]
+
+    def hop_in(o, k, yy, zz):
         return remote(
-            up.at[d_of[o], zz, rows, :], hop.at[o - 2, i], hop_slots[o][i], hand_peer if low else cross_peer[o]
-        )
-
-    def hop_on(o, i):
-        zz, low = i // 2, i % 2 == 0
-        rows = pl.ds(0 if low else 128, 128)
-        home = d if low else d_of[o]
+            up.at[yy, zz, pl.ds(k * 128, 128), :], hop.at[o - 2, k, zz], hop_slots[o][k] + zz,
+            hand_peer if k == 0 else cross_peer[o],
+        )
+
+    def hop_on(o, k, zz):
         return remote(
-            hop.at[o - 2, i], up_g.at[home, rows, pl.ds(zz * TILE, TILE)], up_slots[o],
-            cross_peer[o] if low else hand_peer,
+            hop.at[o - 2, k, zz], up_g.at[d if k == 0 else d_of[o], pl.ds(k * 128, 128), quarter(0, zz)],
+            up_slots[o], cross_peer[o] if k == 0 else hand_peer,
         )
 
     lane = lax.broadcasted_iota(jnp.int32, (SEQ, HD), 1)
@@ -350,18 +376,21 @@
     def halves(k):
         return pl.ds(k * 128, 128)
 
+    def offer(k, yy, zz):
+        for o in (2, 3):
+            @pl.when(yy == d_of[o])
+            def _():
+                hop_in(o, k, yy, zz).start()
+
     def add_context(k, yy, zz):
         dctx[halves(k), :] += dot_nn(up[yy, zz, halves(k), :], wo[wo_rows(yy, zz), :])
 
-    own_slots = [slot() for _ in range(4)]
+    own_slots = [slot() for _ in range(2)]
     p1_slots = [[slot() for _ in range(4)] for _ in range(2)]
     p2_slots = [[[slot() for _ in range(4)] for _ in range(4)] for _ in range(2)]
 
-    def rows_of(g):
-        return pl.ds(g * 64, 64)
-
     def hand_copy(g):
-        return remote(gin.at[rows_of(g), :], up.at[y, z, rows_of(g), :], own_slots[g], hand_peer)
+        return remote(gin.at[halves(g), :], up.at[y, z, halves(g), :], own_slots[g], hand_peer)
 
     def at(k, first, second):
         return (second, first) if k == 0 else (first, second)
@@ -379,12 +408,14 @@
 
         lax.fori_loop(0, 4, body, 0)
 
+    gathered = []
+
     @pl.when(is_earlier)
     def _():
+        share_tok()
         first_of, second_of = (z, y), (y, z)
         first_right, first_left = (z_right, y_right), (z_left, y_left)
         second_right, second_left = (y_right, z_right), (y_left, z_left)
-        pending = []
 
         def piece(k, a, b, lo, n):
             yy, zz = at(k, a, b)
@@ -392,9 +423,8 @@
 
         def send(k, a, b, lo, n, index, peer):
             ref = piece(k, a, b, lo, n)
-            copy = remote(ref, ref, index, peer)
-            copy.start()
-            pending.append(copy)
+            remote(ref, ref, index, peer).start()
+            gathered.append((n, index))
 
         def arrived(k, a, b, lo, n, index):
             ref = piece(k, a, b, lo, n)
@@ -406,12 +436,12 @@
             send(k, a, second_of[k], 0, 128, p2_slots[k][o][1], second_left[k])
 
         for k in range(2):
-            hand_copy(2 * k).wait_recv()
-            hand_copy(2 * k + 1).wait_recv()
+            hand_copy(k).wait_recv()
             send(k, first_of[k], second_of[k], 0, 128, p1_slots[k][0], first_right[k])
             send(k, first_of[k], second_of[k], 0, 128, p1_slots[k][1], first_left[k])
             spread(k, 0)
         for k in range(2):
+            offer(k, y, z)
             add_context(k, y, z)
         for k in range(2):
             a, b = ring(first_of[k] - 1), second_of[k]
@@ -424,6 +454,7 @@
             spread(k, 1)
         for k in range(2):
             for o in (3, 1):
+                offer(k, *at(k, ring(first_of[k] + o), second_of[k]))
                 add_context(k, *at(k, ring(first_of[k] + o), second_of[k]))
 
         def relay(k, o):
@@ -433,8 +464,9 @@
             send(k, a, left, 0, 64, p2_slots[k][o][2], second_right[k])
             arrived(k, a, right, 0, 128, p2_slots[k][o][1])
             send(k, a, right, 64, 64, p2_slots[k][o][3], second_left[k])
-            add_context(k, *at(k, a, left))
-            add_context(k, *at(k, a, right))
+            for b in (left, right):
+                offer(k, *at(k, a, b))
+                add_context(k, *at(k, a, b))
 
         for k in range(2):
             relay(k, 0)
@@ -443,6 +475,7 @@
             arrived(k, a, b, 0, 64, p1_slots[k][2])
             arrived(k, a, b, 64, 64, p1_slots[k][3])
             spread(k, 2)
+            offer(k, *at(k, a, b))
             add_context(k, *at(k, a, b))
         for o in (3, 1, 2):
             for k in range(2):
@@ -452,12 +485,8 @@
                 a, b = ring(first_of[k] + o), ring(second_of[k] + 2)
                 arrived(k, a, b, 0, 64, p2_slots[k][o][2])
                 arrived(k, a, b, 64, 64, p2_slots[k][o][3])
+                offer(k, *at(k, a, b))
                 add_context(k, *at(k, a, b))
-        for copy in pending:
-            copy.wait_send()
-        for i in range(8):
-            for o in (2, 3):
-                hop_send(o, i).start()
 
     for zz in range(4):
         up_send(1, zz).start()
@@ -515,9 +544,9 @@
     right_2, left_2 = (z_right, y_right), (z_left, y_left)
 
     def block(g, a, lo, n):
-        if g < 2:
-            return part.at[a, pl.ds(lo, n), rows_of(g), :]
-        return part.at[pl.ds(lo, n), a, rows_of(g), :]
+        if g == 0:
+            return part.at[a, pl.ds(lo, n), halves(g), :]
+        return part.at[pl.ds(lo, n), a, halves(g), :]
 
     def tile(k, a, b):
         return (a, b) if k == 0 else (b, a)
@@ -530,8 +559,8 @@
             total = total * gain[0:1, span].astype(F32) - tok[:, span].astype(F32) * cs_ref[:, 0:1]
             part[yy, zz] = total.astype(BF16)
 
-    rs1 = [[slot() for _ in range(6)] for _ in range(4)]
-    rs2 = [[slot() for _ in range(6)] for _ in range(4)]
+    rs1 = [[slot() for _ in range(6)] for _ in range(2)]
+    rs2 = [[slot() for _ in range(6)] for _ in range(2)]
 
     def go(src, dst, n, peer):
         copy = remote(src, dst, n, peer)
@@ -542,26 +571,26 @@
         remote(ref, ref, n, y_right).wait_recv()
 
     def relay_1(g):
-        k, i = g // 2, ring_of[g // 2]
+        k, i = g, ring_of[g]
         go(block(g, ring(i + 2), 0, 2), rrel.at[g, 0:2], rs1[g][0], right_1[k])
         go(block(g, ring(i + 2), 2, 2), rrel.at[g, 2:4], rs1[g][1], left_1[k])
 
     def direct_right_1(g):
-        k, i = g // 2, ring_of[g // 2]
+        k, i = g, ring_of[g]
         go(block(g, ring(i + 1), 2, 2), rdir.at[g, 2:4], rs1[g][5], right_1[k])
 
     def direct_left_1(g):
-        k, i = g // 2, ring_of[g // 2]
+        k, i = g, ring_of[g]
         go(block(g, ring(i - 1), 0, 2), rdir.at[g, 0:2], rs1[g][4], left_1[k])
 
     def add_relay(g, a, b):
-        yy, zz = tile(g // 2, a, b)
-        part[yy, zz, rows_of(g), :] = (
-            part[yy, zz, rows_of(g), :].astype(F32) + rrel[g, b].astype(F32)
+        yy, zz = tile(g, a, b)
+        part[yy, zz, halves(g), :] = (
+            part[yy, zz, halves(g), :].astype(F32) + rrel[g, b].astype(F32)
         ).astype(BF16)
 
     def accumulate_1(g):
-        k, i = g // 2, ring_of[g // 2]
+        k, i = g, ring_of[g]
         landed(rrel.at[g, 0:2], rs1[g][0])
         for b in range(2):
             add_relay(g, ring(i + 1), b)
@@ -572,96 +601,88 @@
         go(block(g, ring(i - 1), 2, 2), racc.at[g, 2:4], rs1[g][3], left_1[k])
 
     def collect(g, b):
-        yy, zz = tile(g // 2, ring_of[g // 2], b)
+        yy, zz = tile(g, ring_of[g], b)
         summed[g, b] = (
-            part[yy, zz, rows_of(g), :].astype(F32) + racc[g, b].astype(F32) + rdir[g, b].astype(F32)
+            part[yy, zz, halves(g), :].astype(F32) + racc[g, b].astype(F32) + rdir[g, b].astype(F32)
         ).astype(BF16)
 
     def turn(g):
-        k, j = g // 2, other_of[g // 2]
+        k, j = g, other_of[g]
         landed(rdir.at[g, 0:2], rs1[g][4])
         landed(rdir.at[g, 2:4], rs1[g][5])
         landed(racc.at[g, 0:2], rs1[g][2])
         landed(racc.at[g, 2:4], rs1[g][3])
         collect(g, ring(j + 2))
-        go(summed.at[g, ring(j + 2), 0:32], rrel2.at[g, 0:32], rs2[g][0], right_2[k])
-        go(summed.at[g, ring(j + 2), 32:64], rrel2.at[g, 32:64], rs2[g][1], left_2[k])
+        go(summed.at[g, ring(j + 2), 0:64], rrel2.at[g, 0:64], rs2[g][0], right_2[k])
+        go(summed.at[g, ring(j + 2), 64:128], rrel2.at[g, 64:128], rs2[g][1], left_2[k])
         collect(g, ring(j + 1))
-        go(summed.at[g, ring(j + 1), 32:64], rdir2.at[g, 32:64], rs2[g][5], right_2[k])
+        go(summed.at[g, ring(j + 1), 64:128], rdir2.at[g, 64:128], rs2[g][5], right_2[k])
         collect(g, ring(j - 1))
-        go(summed.at[g, ring(j - 1), 0:32], rdir2.at[g, 0:32], rs2[g][4], left_2[k])
+        go(summed.at[g, ring(j - 1), 0:64], rdir2.at[g, 0:64], rs2[g][4], left_2[k])
         collect(g, j)
 
     def accumulate_2(g):
-        k, j = g // 2, other_of[g // 2]
-        landed(rrel2.at[g, 0:32], rs2[g][0])
+        k, j = g, other_of[g]
+        landed(rrel2.at[g, 0:64], rs2[g][0])
         a = ring(j + 1)
-        summed[g, a, 0:32] = (summed[g, a, 0:32].astype(F32) + rrel2[g, 0:32].astype(F32)).astype(BF16)
-        go(summed.at[g, a, 0:32], racc2.at[g, 0:32], rs2[g][2], right_2[k])
-        landed(rrel2.at[g, 32:64], rs2[g][1])
+        summed[g, a, 0:64] = (summed[g, a, 0:64].astype(F32) + rrel2[g, 0:64].astype(F32)).astype(BF16)
+        go(summed.at[g, a, 0:64], racc2.at[g, 0:64], rs2[g][2], right_2[k])
+        landed(rrel2.at[g, 64:128], rs2[g][1])
         a = ring(j - 1)
-        summed[g, a, 32:64] = (summed[g, a, 32:64].astype(F32) + rrel2[g, 32:64].astype(F32)).astype(BF16)
-        go(summed.at[g, a, 32:64], racc2.at[g, 32:64], rs2[g][3], left_2[k])
+        summed[g, a, 64:128] = (summed[g, a, 64:128].astype(F32) + rrel2[g, 64:128].astype(F32)).astype(BF16)
+        go(summed.at[g, a, 64:128], racc2.at[g, 64:128], rs2[g][3], left_2[k])
 
     def result(g):
-        j = other_of[g // 2]
-        landed(rdir2.at[g, 0:32], rs2[g][4])
-        landed(rdir2.at[g, 32:64], rs2[g][5])
-        landed(racc2.at[g, 0:32], rs2[g][2])
-        landed(racc2.at[g, 32:64], rs2[g][3])
-        gin[rows_of(g), :] = (
-            up[y, z, rows_of(g), :].astype(F32)
+        j = other_of[g]
+        landed(rdir2.at[g, 0:64], rs2[g][4])
+        landed(rdir2.at[g, 64:128], rs2[g][5])
+        landed(racc2.at[g, 0:64], rs2[g][2])
+        landed(racc2.at[g, 64:128], rs2[g][3])
+        gin[halves(g), :] = (
+            up[y, z, halves(g), :].astype(F32)
             + summed[g, j].astype(F32)
             + racc2[g].astype(F32)
             + rdir2[g].astype(F32)
         ).astype(BF16)
         pl.when(is_later)(lambda: hand_copy(g).start())
 
-    def each(step, *groups):
-        for g in groups:
-            step(g)
-
     compute((2, 2), (2, 1), (2, 3), (2, 0))
-    each(relay_1, 0, 1)
+    relay_1(0)
     compute((1, 2), (3, 2), (0, 2))
-    each(relay_1, 2, 3)
+    relay_1(1)
     compute((1, 1), (1, 3), (1, 0))
     direct_right_1(0)
     compute((3, 1), (3, 3), (3, 0))
     direct_left_1(0)
     compute((0, 1), (0, 3))
-    each(direct_right_1, 2)
-    each(direct_left_1, 2)
-    each(accumulate_1, 0, 2)
-    each(direct_right_1, 1, 3)
-    each(direct_left_1, 1, 3)
+    direct_right_1(1)
+    direct_left_1(1)
     compute((0, 0))
-    each(accumulate_1, 1, 3)
-    each(turn, 0, 2)
-    each(accumulate_2, 0, 2)
-    each(turn, 1, 3)
-    each(result, 0, 2)
-    each(accumulate_2, 1, 3)
-    each(result, 1, 3)
+    for step in (accumulate_1, turn, accumulate_2, result):
+        step(0)
+        step(1)
 
     @pl.when(is_later)
     def _():
+        share_tok()
         for o in (2, 3):
             cot_quarter(o).wait_recv()
             for p in (1, 2, 3):
                 cot_share(o, p).start()
             cot_keep(o).start()
-        for i in range(8):
-            for o in (2, 3):
-                hop_send(o, i).wait_recv()
-                hop_on(o, i).start()
-        for g in range(4):
+        for dz in (0, 3, 1, 2):
+            for k in range(2):
+                for o in (2, 3):
+                    zz = ring(z + dz)
+                    hop_in(o, k, 0, zz).wait_recv()
+                    hop_on(o, k, zz).start()
+        for g in range(2):
             hand_copy(g).wait_send()
 
     finish()
 
 
-N_SLOTS = 6 + 3 + 2 + 6 + 16 + 3 + 4 + 8 + 32 + 3 + 3 + 48
+N_SLOTS = 6 + 3 + 2 + 12 + 16 + 3 + 2 + 8 + 32 + 3 + 3 + 24
 
 
 def relay(late, cot, early, lens, gain, w_q, w_k, w_v, w_o, freq):
@@ -700,21 +721,22 @@
         pltpu.VMEM((SEQ, KV), BF16),
         pltpu.VMEM((ROWS, SEQ), BF16),
         pltpu.VMEM((256, SEQ), BF16),
-        pltpu.VMEM((4, 4, 64, TILE), BF16),
-        pltpu.VMEM((4, 4, 64, TILE), BF16),
-        pltpu.VMEM((4, 4, 64, TILE), BF16),
-        pltpu.VMEM((4, 4, 64, TILE), BF16),
-        pltpu.VMEM((4, 64, TILE), BF16),
-        pltpu.VMEM((4, 64, TILE), BF16),
-        pltpu.VMEM((4, 64, TILE), BF16),
-        pltpu.VMEM((2, 8, 128, TILE), BF16),
-        pltpu.VMEM((2, SEQ, BLOCK), BF16),
+        pltpu.VMEM((2, 4, 128, TILE), BF16),
+        pltpu.VMEM((2, 4, 128, TILE), BF16),
+        pltpu.VMEM((2, 4, 128, TILE), BF16),
+        pltpu.VMEM((2, 4, 128, TILE), BF16),
+        pltpu.VMEM((2, 128, TILE), BF16),
+        pltpu.VMEM((2, 128, TILE), BF16),
+        pltpu.VMEM((2, 128, TILE), BF16),
+        pltpu.VMEM((2, 2, 4, 128, TILE), BF16),
+        pltpu.VMEM((2, SEQ, TILE), BF16),
+        pltpu.VMEM((2, SEQ, TILE), BF16),
         pltpu.VMEM((2, SEQ, TILE), BF16),
         pltpu.VMEM((2, SEQ, TILE), BF16),
         pltpu.SemaphoreType.DMA((5, N_CHUNK)),
         pltpu.SemaphoreType.DMA((4, 4)),
         pltpu.SemaphoreType.DMA((2, 2)),
-        pltpu.SemaphoreType.DMA((6,)),
+        pltpu.SemaphoreType.DMA((8,)),
         pltpu.SemaphoreType.DMA((N_SLOTS,)),
         pltpu.SemaphoreType.DMA((N_SLOTS,)),
     ]

time: 126 us -> 118 us (0.937); the launches traced: 124 us -> 118 us
  Pallas kernels: 123 us -> 118 us
    pallas_call x1, Pallas kernels: 116 us -> 110 us  [relay(): pl.pallas_call(relay_kernel, out_shape=out_shape, in_specs=[any_spec, any...]
where the time goes in v3:
time: 118 us
  Pallas kernels  118 us (100%)
    pallas_call x1, Pallas kernels, relay(): pl.pallas_call(relay_kernel, out_shape=out_shape, in_specs=[any_spec, any...  110 us
    pallas_call x1, Pallas kernels, weight_grads(): pl.pallas_call(weights_kernel, grid=(4,), out_shape=(jax.ShapeDtypeStruct...  7.13 us

profile of v3, /device:TPU:0, one launch (start us, length us, event | category | flops | bytes accessed | tf_op | source)
XLA Modules:
  0.0 118.2 jit_solution(3821577942587681051)
XLA Ops:
  0.6 110.4 %relay.1 = (bf16[256,512]{1,0:T(8,128)(2,1)}, bf16[4,256,2048]{2,1,0:T(8,128)(2,1)}, bf16[4,256,2048]{2,1,0:T(8,128)(2,1)}, bf16[4,320,256]{2,1,0:T(8,128)(2,1)}, bf16[4,256,256]{2,1,0:T(8,128)(2,1)}) custom-call(bf16[256,8192]{1,0:T(8,128)(2,1)} %late.1, bf16[256,8192]{1,0:T(8,128)(2,1)} %cot.1, bf16[256,8192]{1,0:T(8,128)(2,1)} %early.1, s32[1,4]{1,0:T(1,128)} %lens.1, ...), custom_call_target="tpu_custom_call" | custom-call | tf_op jit(solution)/shard_map/relay/pallas_call | solution.py:743
  111.1 7.1 %weight_grads.1 = (bf16[2048,256]{1,0:T(8,128)(2,1)}, bf16[2048,256]{1,0:T(8,128)(2,1)}, bf16[32,2048]{1,0:T(8,128)(2,1)}, bf16[32,2048]{1,0:T(8,128)(2,1)}, bf16[256,512]{1,0:T(8,128)(2,1)}) custom-call(bf16[4,256,2048]{2,1,0:T(8,128)(2,1)} %get-tuple-element.15.tok, bf16[4,256,2048]{2,1,0:T(8,128)(2,1)} %get-tuple-element.16.up, ...), custom_call_target="tpu_custom_call" | custom-call | tf_op jit(solution)/shard_map/weight_grads/pallas_call | solution.py:774

commit v4 on v3

--- a/solution.py
+++ b/solution.py
@@ -15,9 +15,11 @@
 TILE = 512
 BLOCK = 2048
 KV = 64
+STEP = 1024
 ROWS = 320
 CHUNK = 1024
 N_CHUNK = D // CHUNK
+FIRST_TILES = [(2, 2), (2, 1), (2, 3), (2, 0), (1, 2), (3, 2), (0, 2)]
 SCALE = 1.0 / math.sqrt(HD)
 F32 = jnp.float32
 BF16 = jnp.bfloat16
@@ -54,7 +56,7 @@
     gin, tok_g, up_g, d_g, c_g,
     tok, wq, wkv, wo, up, part,
     xq, xkv, dctx, probs, dss, qs, qs_t, kv_all, kvp_send, kvp_recv, cosv, sinv, inv_ref, cs_ref,
-    aq, akv, dqkv, ctx,
+    aq, akv, dqkv, ctx, early_sum,
     rrel, racc, rdir, summed, rrel2, racc2, rdir2, hop, tok_stage, tok_part, cot_stage, cot_part,
     load_sem, up_sem, stage_sem, loc_sem, send_sem, recv_sem,
 ):
@@ -341,6 +343,26 @@
         qs[j] = q.astype(BF16)
         qs_t[j] = jnp.transpose(q).astype(BF16)
     inv_t = jnp.transpose(inv_ref[...])[0:1, :]
+    for i in range(N_CHUNK):
+        wo_copy(i).wait()
+    dctx[...] = jnp.zeros_like(dctx)
+
+    def wo_rows(yy, zz):
+        return pl.ds(pl.multiple_of((yy * 4 + zz) * TILE, TILE), TILE)
+
+    @pl.when(is_later)
+    def _():
+        def body(yy, carry):
+            total = dctx[...]
+            for zz in range(4):
+                cot_copy(yy, zz).wait()
+            for zz in range(4):
+                total += dot_nn(up[yy, zz], wo[wo_rows(yy, zz), :])
+            dctx[...] = total
+            return carry
+
+        lax.fori_loop(0, 4, body, 0)
+
     for copy in kv_copies:
         copy.wait_recv()
     k = jnp.concatenate([kv_all[i, 0:32] for i in range(4)], axis=0).astype(F32)
@@ -357,22 +379,16 @@
         pr = ex / jnp.sum(ex, axis=1, keepdims=True)
         probs[j] = pr
         ctx[j * HD:(j + 1) * HD, :] = dot_nt(v_t, pr.astype(BF16)).astype(BF16)
+    own_cols = pl.ds(pl.multiple_of(d * SEQ, SEQ), SEQ)
     ctx_slots = [None] + [slot() for _ in range(3)]
-    ctx_copies = [remote(ctx, c_g.at[d], ctx_slots[o], dp_peer[o]) for o in (1, 2, 3)]
-    ctx_keep = pltpu.make_async_copy(ctx, c_g.at[d], loc_sem.at[2])
+    ctx_copies = [remote(ctx, c_g.at[:, own_cols], ctx_slots[o], dp_peer[o]) for o in (1, 2, 3)]
+    ctx_keep = pltpu.make_async_copy(ctx, c_g.at[:, own_cols], loc_sem.at[2])
     for copy in ctx_copies:
         copy.start()
     ctx_keep.start()
     received += ctx_copies + [ctx_keep]
     send_operands()
 
-    for i in range(N_CHUNK):
-        wo_copy(i).wait()
-    dctx[...] = jnp.zeros_like(dctx)
-
-    def wo_rows(yy, zz):
-        return pl.ds(pl.multiple_of((yy * 4 + zz) * TILE, TILE), TILE)
-
     def halves(k):
         return pl.ds(k * 128, 128)
 
@@ -394,19 +410,6 @@
 
     def at(k, first, second):
         return (second, first) if k == 0 else (first, second)
-
-    @pl.when(is_later)
-    def _():
-        def body(yy, carry):
-            total = dctx[...]
-            for zz in range(4):
-                cot_copy(yy, zz).wait()
-            for zz in range(4):
-                total += dot_nn(up[yy, zz], wo[wo_rows(yy, zz), :])
-            dctx[...] = total
-            return carry
-
-        lax.fori_loop(0, 4, body, 0)
 
     gathered = []
 
@@ -521,6 +524,8 @@
     dq = jnp.transpose(dq_t)
     aq[...] = (dq * inv).astype(BF16)
     stat = jnp.sum(dq * xq[...], axis=1, keepdims=True)
+    for n, (dy, dz) in enumerate(FIRST_TILES):
+        early_sum[n] = dot_nt(aq[...], wq[wo_rows(ring(y + dy), ring(z + dz)), :])
     for copy in kvp_copies:
         copy.wait_recv()
     dkv_t = kvp_send[z].astype(F32)
@@ -532,8 +537,8 @@
     stat += jnp.sum(dkv * xkv[...], axis=1, keepdims=True)
     cs_ref[...] = jnp.broadcast_to(inv * inv * inv * stat * (1.0 / D), cs_ref.shape)
     d_slots = [None] + [slot() for _ in range(3)]
-    d_copies = [remote(dqkv, d_g.at[d], d_slots[o], dp_peer[o]) for o in (1, 2, 3)]
-    d_keep = pltpu.make_async_copy(dqkv, d_g.at[d], loc_sem.at[3])
+    d_copies = [remote(dqkv, d_g.at[:, own_cols], d_slots[o], dp_peer[o]) for o in (1, 2, 3)]
+    d_keep = pltpu.make_async_copy(dqkv, d_g.at[:, own_cols], loc_sem.at[3])
     for copy in d_copies:
         copy.start()
     d_keep.start()
@@ -555,7 +560,11 @@
         for dy, dz in tiles:
             yy, zz = ring(y + dy), ring(z + dz)
             span = wo_rows(yy, zz)
-            total = dot_nt(aq[...], wq[span, :]) + dot_nn(akv[...], wkv[:, span])
+            total = dot_nn(akv[...], wkv[:, span])
+            if (dy, dz) in FIRST_TILES:
+                total += early_sum[FIRST_TILES.index((dy, dz))]
+            else:
+                total += dot_nt(aq[...], wq[span, :])
             total = total * gain[0:1, span].astype(F32) - tok[:, span].astype(F32) * cs_ref[:, 0:1]
             part[yy, zz] = total.astype(BF16)
 
@@ -693,8 +702,8 @@
         jax.ShapeDtypeStruct((SEQ, TILE), BF16),
         jax.ShapeDtypeStruct((4, SEQ, BLOCK), BF16),
         jax.ShapeDtypeStruct((4, SEQ, BLOCK), BF16),
-        jax.ShapeDtypeStruct((4, ROWS, SEQ), BF16),
-        jax.ShapeDtypeStruct((4, SEQ, SEQ), BF16),
+        jax.ShapeDtypeStruct((ROWS, 4 * SEQ), BF16),
+        jax.ShapeDtypeStruct((SEQ, 4 * SEQ), BF16),
     )
     scratch = [
         pltpu.VMEM((SEQ, D), BF16),
@@ -721,6 +730,7 @@
         pltpu.VMEM((SEQ, KV), BF16),
         pltpu.VMEM((ROWS, SEQ), BF16),
         pltpu.VMEM((256, SEQ), BF16),
+        pltpu.VMEM((len(FIRST_TILES), SEQ, TILE), F32),
         pltpu.VMEM((2, 4, 128, TILE), BF16),
         pltpu.VMEM((2, 4, 128, TILE), BF16),
         pltpu.VMEM((2, 4, 128, TILE), BF16),
@@ -755,17 +765,13 @@
 
 def weights_kernel(tok, up, d_ref, c_ref, gain, gin, q_out, o_out, k_out, v_out, gin_out):
     i = pl.program_id(0)
-    start = pl.multiple_of(lax.axis_index("dp") * BLOCK + i * TILE, TILE)
-    total = dot_nn(d_ref[0], tok[0])
-    for e in range(1, 4):
-        total += dot_nn(d_ref[e], tok[e])
-    total = total * gain[0:1, pl.ds(start, TILE)].astype(F32)
+    start = pl.multiple_of(lax.axis_index("dp") * BLOCK + i * STEP, STEP)
+    total = dot_nn(d_ref[...], tok[...].reshape(4 * SEQ, STEP))
+    total = total * gain[0:1, pl.ds(start, STEP)].astype(F32)
     q_out[...] = jnp.transpose(total[0:256]).astype(BF16)
     k_out[...] = total[256:288].astype(BF16)
     v_out[...] = total[288:320].astype(BF16)
-    other = dot_nn(c_ref[0], up[0])
-    for e in range(1, 4):
-        other += dot_nn(c_ref[e], up[e])
+    other = dot_nn(c_ref[...], up[...].reshape(4 * SEQ, STEP))
     o_out[...] = jnp.transpose(other).astype(BF16)
     gin_out[...] = gin[...]
 
@@ -773,7 +779,7 @@
 def weight_grads(tok_g, up_g, d_g, c_g, gain, gin):
     return pl.pallas_call(
         weights_kernel,
-        grid=(4,),
+        grid=(BLOCK // STEP,),
         out_shape=(
             jax.ShapeDtypeStruct((BLOCK, 256), BF16),
             jax.ShapeDtypeStruct((BLOCK, 256), BF16),
@@ -782,18 +788,18 @@
             jax.ShapeDtypeStruct((SEQ, TILE), BF16),
         ),
         in_specs=[
-            pl.BlockSpec((4, SEQ, TILE), lambda i: (0, 0, i)),
-            pl.BlockSpec((4, SEQ, TILE), lambda i: (0, 0, i)),
-            pl.BlockSpec((4, ROWS, SEQ), lambda i: (0, 0, 0)),
-            pl.BlockSpec((4, SEQ, SEQ), lambda i: (0, 0, 0)),
+            pl.BlockSpec((4, SEQ, STEP), lambda i: (0, 0, i)),
+            pl.BlockSpec((4, SEQ, STEP), lambda i: (0, 0, i)),
+            pl.BlockSpec((ROWS, 4 * SEQ), lambda i: (0, 0)),
+            pl.BlockSpec((SEQ, 4 * SEQ), lambda i: (0, 0)),
             pl.BlockSpec((1, D), lambda i: (0, 0)),
             pl.BlockSpec((SEQ, TILE), lambda i: (0, 0)),
         ],
         out_specs=(
-            pl.BlockSpec((TILE, 256), lambda i: (i, 0)),
-            pl.BlockSpec((TILE, 256), lambda i: (i, 0)),
-            pl.BlockSpec((32, TILE), lambda i: (0, i)),
-            pl.BlockSpec((32, TILE), lambda i: (0, i)),
+            pl.BlockSpec((STEP, 256), lambda i: (i, 0)),
+            pl.BlockSpec((STEP, 256), lambda i: (i, 0)),
+            pl.BlockSpec((32, STEP), lambda i: (0, i)),
+            pl.BlockSpec((32, STEP), lambda i: (0, i)),
             pl.BlockSpec((SEQ, TILE), lambda i: (0, 0)),
         ),
         compiler_params=pltpu.CompilerParams(vmem_limit_bytes=62 * 1024 * 1024),

time: 118 us -> 118 us (level)
  no operation moved by 1% of the time
where the time goes in v4:
time: 118 us
  Pallas kernels  117 us (99%)
    pallas_call x1, Pallas kernels, relay(): pl.pallas_call(relay_kernel, out_shape=out_shape, in_specs=[any_spec, any...  111 us
    pallas_call x1, Pallas kernels, weight_grads(): pl.pallas_call(weights_kernel, grid=(BLOCK // STEP,), out_shape=(jax.Shap...  6.43 us

profile of v4, /device:TPU:0, one launch (start us, length us, event | category | flops | bytes accessed | tf_op | source)
XLA Modules:
  0.0 117.8 jit_solution(12872443066695375490)
XLA Ops:
  0.6 110.7 %relay.1 = (bf16[256,512]{1,0:T(8,128)(2,1)}, bf16[4,256,2048]{2,1,0:T(8,128)(2,1)}, bf16[4,256,2048]{2,1,0:T(8,128)(2,1)}, bf16[320,1024]{1,0:T(8,128)(2,1)}, bf16[256,1024]{1,0:T(8,128)(2,1)}) custom-call(bf16[256,8192]{1,0:T(8,128)(2,1)} %late.1, bf16[256,8192]{1,0:T(8,128)(2,1)} %cot.1, bf16[256,8192]{1,0:T(8,128)(2,1)} %early.1, s32[1,4]{1,0:T(1,128)} %lens.1, ...), custom_call_target="tpu_custom_call" | custom-call | tf_op jit(solution)/shard_map/relay/pallas_call | solution.py:753
  111.4 6.4 %weight_grads.1 = (bf16[2048,256]{1,0:T(8,128)(2,1)}, bf16[2048,256]{1,0:T(8,128)(2,1)}, bf16[32,2048]{1,0:T(8,128)(2,1)}, bf16[32,2048]{1,0:T(8,128)(2,1)}, bf16[256,512]{1,0:T(8,128)(2,1)}) custom-call(bf16[4,256,2048]{2,1,0:T(8,128)(2,1)} %get-tuple-element.15.tok, bf16[4,256,2048]{2,1,0:T(8,128)(2,1)} %get-tuple-element.16.up, ...), custom_call_target="tpu_custom_call" | custom-call | tf_op jit(solution)/shard_map/weight_grads/pallas_call | solution.py:780
